TPU v7x, 512 devices: a whole 4x4x16 slice. The times are simulated.
512 devices in a mesh: pts: 128 (over x_lo, z, y), dim: 4 (over x_hi, core).
Axes of the slice: x: 4 (x_hi: 2, x_lo: 2; x = x_hi * 2 + x_lo), y: 4, z: 16, core: 2. Of those that a mesh axis runs over, the one named last changes fastest.
Arguments:
- factors: bfloat16 [8, 262144, 256], P('dim', 'pts'), may hold values from -6 to 6
- tridiag: bfloat16 [8, 256, 256], P('dim'), may hold values from -0.5 to 1.5, as said below
- probe_vector: float32 [262144], P('pts'), may hold values from -0.03125 to 0.03125
- cotangent: float32 [4, 262144], P(None, 'pts'), may hold values from -1 to 1
Outputs:
- grad_factors: bfloat16 [8, 262144, 256], P('dim', 'pts')
Inputs may be any that keep to these rules, and one draw needn't show every extreme that they name: `tridiag`: each T_d is symmetric tridiagonal with a dominant diagonal.
All inputs are finite; a program needn't handle non-finite values.
Results may differ from a plain program's by a relative error of at most 0.007.
Values may be sent and summed in bfloat16 or wider, within the bound.
No kernel may reach another device: no remote copies, remote signals or barrier semaphores. Data moves between devices by JAX's collectives and lax.ppermute only.
A program may use at most 64 MiB of HBM per device.

v0:
```python
import jax
import jax.numpy as jnp
from jax import lax
from jax.sharding import PartitionSpec as P


def partner(block, axis, apart):
    count = lax.axis_size(axis)
    route = []
    for low in range(count):
        high = low | 1 << apart
        if high != low and high < count:
            route += [(low, high), (high, low)]
    return lax.ppermute(block, axis, route)


def per_device(factors, tridiag, probe_vector, cotangent):
    count = lax.axis_size("dim")
    half = count // 2
    bit = count.bit_length() - 2
    owner = lax.axis_index("dim")
    is_upper = owner >= half
    local_dims = factors.shape[0]
    start = owner % half * local_dims
    cot = lax.dynamic_slice_in_dim(cotangent, start, local_dims, 0)
    own_prod = jnp.einsum(
        "dnr,drs->dns", factors, tridiag, preferred_element_type=jnp.float32
    ).astype(jnp.bfloat16)
    other_q, other_t = partner((factors, tridiag), "dim", bit)
    other_prod = jnp.einsum(
        "dnr,drs->dns", other_q, other_t, preferred_element_type=jnp.float32
    ).astype(jnp.bfloat16)
    q_first = jnp.where(is_upper, other_q, factors)
    q_second = jnp.where(is_upper, factors, other_q)
    p_first = jnp.where(is_upper, other_prod, own_prod)
    p_second = jnp.where(is_upper, own_prod, other_prod)
    scaled_q = (probe_vector[None, :, None] * q_second).astype(jnp.bfloat16)
    scaled_p = (cot[:, :, None] * p_second).astype(jnp.bfloat16)
    m_part = jnp.einsum("dnr,dns->drs", q_first, scaled_q, preferred_element_type=jnp.float32)
    g_part = jnp.einsum("dnr,dns->drs", p_first, scaled_p, preferred_element_type=jnp.float32)
    m_total, g_total = lax.psum((m_part, g_part), "pts")
    m_round = m_total.astype(jnp.bfloat16)
    g_round = g_total.astype(jnp.bfloat16)
    m_flip = jnp.transpose(m_round, (0, 2, 1))
    g_flip = jnp.transpose(g_round, (0, 2, 1))
    m_use = jnp.where(is_upper, m_flip, m_round)
    g_use = jnp.where(is_upper, g_flip, g_round)
    lifted = jnp.einsum("dns,drs->dnr", other_prod, m_use, preferred_element_type=jnp.float32)
    grad_prod = (cot[:, :, None] * lifted).astype(jnp.bfloat16)
    through_t = jnp.einsum("dns,drs->dnr", grad_prod, tridiag, preferred_element_type=jnp.float32)
    through_gram = jnp.einsum("dns,drs->dnr", other_q, g_use, preferred_element_type=jnp.float32)
    return (through_t + probe_vector[None, :, None] * through_gram).astype(jnp.bfloat16)


def solution(mesh):
    return jax.shard_map(
        per_device,
        mesh=mesh,
        in_specs=(P("dim", "pts", None), P("dim", None, None), P("pts"), P(None, "pts")),
        out_specs=P("dim", "pts", None),
        check_vma=False,
    )
```

profile of v0, /device:TPU:6, one launch (start us, length us, event | category | flops | bytes accessed | tf_op | source)
XLA Modules:
  0.0 694.2 jit_solution(18074789144191848733)
XLA Ops:
  0.0 0.0 copy-start
  0.0 3.4 collective-permute-start
  3.4 4.0 collective-permute-start.1
  7.5 3.6 convolution_convert_fusion
  11.1 0.0 copy-done
  11.1 0.0 copy-start.3
  11.1 45.6 %collective-permute-done.1 = bf16[2,256,256]{2,1,0:T(8,128)(2,1)S(1)} collective-permute-done((bf16[2,256,256]{2,1,0:T(8,128)(2,1)}, bf16[2,256,256]{2,1,0:T(8,128)(2,1)S(1)}, u32[]{:S(2)}, u32[]{:S(2)}) %collective-permute-start.1) | collective-permute-done | bytes 262176 | tf_op jit(solution)/shard_map/ppermute | solution.py:14
  56.7 0.0 collective-permute-done
  56.7 0.7 convolution_convert_fusion.1
  57.4 0.0 copy-done.3
  57.4 0.0 copy-start.1
  57.5 0.0 copy-start.2
  57.5 0.0 copy-start.5
  57.5 1.8 fusion.2
  59.3 0.0 copy-done.1
  59.3 0.5 copy-done.2
  59.8 0.0 copy-done.5
  59.8 2.5 fusion.1
  62.3 622.5 %all-reduce.2 = (bf16[2,256,256]{2,1,0:T(8,128)(2,1)S(1)}, bf16[2,256,256]{2,1,0:T(8,128)(2,1)S(1)}) all-reduce(f32[2,256,256]{2,1,0:T(8,128)} %fusion.1, f32[2,256,256]{2,1,0:T(8,128)S(1)} %fusion.2), channel_id=1, replica_groups=mesh['pts'=128,'dim'=4] {'pts'}, use_global_device_ids=true, to_apply=%region_0.1 | all-reduce | flops 262144 | bytes 1572864 | tf_op jit(solution)/shard_map/psum | solution.py:41
  684.8 0.1 copy.6
  684.9 0.0 copy-done.4
  684.9 4.8 fusion.11
  689.8 0.1 copy.8
  689.9 4.3 fusion
  (2 shorter events, 0.0 us)
Async XLA Ops:
  0.0 11.1 %copy-start = (f32[4,2048]{1,0:T(4,128)S(1)}, f32[4,2048]{1,0:T(4,128)}, u32[]{:S(2)}) copy-start(f32[4,2048]{1,0:T(4,128)} %param.7) | copy-start | bytes 98308
  0.0 56.7 %collective-permute-start = (bf16[2,2048,256]{2,1,0:T(8,128)(2,1)}, bf16[2,2048,256]{2,1,0:T(8,128)(2,1)S(1)}, u32[]{:S(2)}, u32[]{:S(2)}) collective-permute-start(bf16[2,2048,256]{2,1,0:T(8,128)(2,1)} %param.4), channel_id=1, source_target_pairs={{0,2},{2,0},{1,3},{3,1},{4,6},{6,4},{5,7},{7,5},{8,10},{10,8},{9,1... | collective-permute-start | bytes 6291464 | tf_op jit(solution)/shard_map/ppermute | solution.py:14
  3.4 53.3 %collective-permute-start.1 = (bf16[2,256,256]{2,1,0:T(8,128)(2,1)}, bf16[2,256,256]{2,1,0:T(8,128)(2,1)S(1)}, u32[]{:S(2)}, u32[]{:S(2)}) collective-permute-start(bf16[2,256,256]{2,1,0:T(8,128)(2,1)} %param.5), channel_id=1, source_target_pairs={{0,2},{2,0},{1,3},{3,1},{4,6},{6,4},{5,7},{7,5},{8,10},{10,8},{9,1... | collective-permute-start | bytes 786440 | tf_op jit(solution)/shard_map/ppermute | solution.py:14
  11.1 46.3 %copy-start.3 = (bf16[2,2048,256]{2,1,0:T(8,128)(2,1)S(1)}, bf16[2,2048,256]{2,1,0:T(8,128)(2,1)}, u32[]{:S(2)}) copy-start(bf16[2,2048,256]{2,1,0:T(8,128)(2,1)} %convolution_convert_fusion) | copy-start | bytes 6291460
  57.4 1.9 copy-start.1
  57.5 2.4 copy-start.2
  57.5 2.3 copy-start.5
  59.8 625.1 %copy-start.4 = (bf16[2,256,256]{2,1,0:T(8,128)(2,1)S(1)}, bf16[2,256,256]{2,1,0:T(8,128)(2,1)}, u32[]{:S(2)}) copy-start(bf16[2,256,256]{2,1,0:T(8,128)(2,1)} %param.5) | copy-start | bytes 786436
where the time goes:
time: 695 us; the launch traced here: 694 us
  blocking collectives  622 us (89%)
  waiting for transfers between devices  45.6 us (7%)
  matrix products  17.7 us (3%)
  starting transfers between devices  7.47 us (1%)
    psum x1, blocking collectives, per_device(): m_total, g_total = lax.psum((m_part, g_part), 'pts')  622 us
    ppermute x2, waiting for transfers between devices, partner(): return lax.ppermute(block, axis, route)  45.6 us
  transfers between devices with their start and end apart: 2, of which 1 were waited for; matrix products, arithmetic and copies ran while one was open for 1% of the time, Pallas kernels for 0%

commit v1 on v0

v1 whole, which is shorter than its diff:
```python
import jax
import jax.numpy as jnp
from jax import lax
from jax.experimental import pallas as pl
from jax.experimental.pallas import tpu as pltpu
from jax.sharding import Mesh, PartitionSpec as P

BF = jnp.bfloat16
F32 = jnp.float32
PARAMS = pltpu.CompilerParams(vmem_limit_bytes=40 * 1024 * 1024)
SWAP = [(0, 1), (1, 0)]
REDUCE = ("z1", "xl", "y")
RING = "zh"
SPREAD = ("xh", "z1", "xl", "y")
STEPS = 4


def exchange(x, axes):
    return lax.all_to_all(x, axes, 0, 0, tiled=True)


def prepare(pos, q, t, v, c, left, send0, send1, send2, scale):
    q_own = q[0]
    rows = q_own.shape[0]
    send0[...] = q_own[: rows // 4]
    send1[...] = q_own[rows // 4 : rows // 2]
    send2[...] = q_own[rows // 2 :]
    prod = lax.dot_general(t[0], q_own, (((1,), (1,)), ((), ())), preferred_element_type=F32)
    prod = prod.astype(BF).astype(F32)
    rank = prod.shape[0]
    first = pos[1] * 2
    c_own = c[pl.ds(first + pos[0], 1), :]
    by_v = (prod * v[...]).astype(BF)
    by_c = (prod * c_own).astype(BF)
    width = rows // STEPS
    for k in range(STEPS):
        left[k, :rank] = by_v[:, k * width : (k + 1) * width]
        left[k, rank:] = by_c[:, k * width : (k + 1) * width]
    row = lax.broadcasted_iota(jnp.int32, (128, rows), 0)
    stack = jnp.where(row == 0, v[...], jnp.where(row == 1, c[pl.ds(first, 1), :], c[pl.ds(first + 1, 1), :]))
    scale[...] = stack.T


def gram(pos, left, q, out, acc):
    step = pl.program_id(0)

    @pl.when(step == 0)
    def _():
        acc[...] = jnp.zeros_like(acc)

    acc[...] += jnp.dot(left[0], q[0], preferred_element_type=F32)

    @pl.when(step == STEPS - 1)
    def _():
        parts, kinds, rows, rank = out.shape
        total = acc[...].astype(BF)
        for kind in range(kinds):
            for part in range(parts):
                at = kind * rank + part * rows
                out[part, kind] = total[at : at + rows]


def add_up(x, out):
    total = x[0].astype(F32)
    for k in range(1, x.shape[0]):
        total = total + x[k].astype(F32)
    total = total.astype(BF)
    for k in range(out.shape[0]):
        out[k] = total


def add_up_through(pos, x, t, out):
    total = x[0].astype(F32)
    for k in range(1, x.shape[0]):
        total = total + x[k].astype(F32)
    kinds, rows, rank = total.shape
    flat = total.reshape(kinds * rows, rank)
    high = flat.astype(BF)
    low = (flat - high.astype(F32)).astype(BF)
    res = jnp.dot(high, t[0], preferred_element_type=F32) + jnp.dot(low, t[0], preferred_element_type=F32)
    res = res.astype(BF).reshape(kinds, rows, rank)
    for k in range(out.shape[0]):
        out[k] = res


def finish(pos, mats, q_near, q_far0, q_far1, q_far2, scale, out):
    step = pl.program_id(0)
    near = pos[0]
    far = 1 - near
    slots, parts, kinds, rows, rank = mats.shape
    v = scale[:, 0:1]
    first = scale[:, 1:2]
    second = scale[:, 2:3]
    c_near = jnp.where(near == 0, first, second)
    c_far = jnp.where(near == 0, second, first)

    def pick(slot, kind):
        return mats[slot, :, kind].reshape(parts * rows, rank)

    def across(q, m):
        return lax.dot_general(q, m, (((1,), (1,)), ((), ())), preferred_element_type=F32)

    q = q_near[0]
    res = c_near * across(q, pick(near, 0)) + v * across(q, pick(near, 1))
    out[near] = res.astype(BF)

    def straight(q):
        a = jnp.dot(q, pick(far, 0), preferred_element_type=F32)
        b = jnp.dot(q, pick(far, 1), preferred_element_type=F32)
        out[far] = (c_far * a + v * b).astype(BF)

    @pl.when(step == 0)
    def _():
        straight(q_far0[...])

    @pl.when(step == 1)
    def _():
        straight(q_far1[...])

    @pl.when(step >= 2)
    def _():
        straight(q_far2[...])


def per_device(factors, tridiag, probe_vector, cotangent):
    dims, rows, rank = factors.shape
    quarter = rows // STEPS
    reducers = lax.axis_size(REDUCE)
    ring = lax.axis_size(RING)
    spread = lax.axis_size(SPREAD)
    piece = rank // reducers
    pos = jnp.stack([lax.axis_index("xh"), lax.axis_index("core")]).astype(jnp.int32)
    v = probe_vector.reshape(1, rows)

    met = exchange(factors, "xh")
    left, send0, send1, send2, scale = pl.pallas_call(
        prepare,
        grid_spec=pltpu.PrefetchScalarGridSpec(
            num_scalar_prefetch=1,
            grid=(1,),
            in_specs=[
                pl.BlockSpec((1, rows, rank), lambda i, s: (s[0], 0, 0)),
                pl.BlockSpec((1, rank, rank), lambda i, s: (s[0], 0, 0)),
                pl.BlockSpec((1, rows), lambda i, s: (0, 0)),
                pl.BlockSpec(cotangent.shape, lambda i, s: (0, 0)),
            ],
            out_specs=[
                pl.BlockSpec((STEPS, 2 * rank, quarter), lambda i, s: (0, 0, 0)),
                pl.BlockSpec((quarter, rank), lambda i, s: (0, 0)),
                pl.BlockSpec((quarter, rank), lambda i, s: (0, 0)),
                pl.BlockSpec((2 * quarter, rank), lambda i, s: (0, 0)),
                pl.BlockSpec((rows, 128), lambda i, s: (0, 0)),
            ],
        ),
        out_shape=[
            jax.ShapeDtypeStruct((STEPS, 2 * rank, quarter), BF),
            jax.ShapeDtypeStruct((quarter, rank), BF),
            jax.ShapeDtypeStruct((quarter, rank), BF),
            jax.ShapeDtypeStruct((2 * quarter, rank), BF),
            jax.ShapeDtypeStruct((rows, 128), F32),
        ],
        compiler_params=PARAMS,
        name="prepare",
    )(pos, factors, tridiag, v, cotangent)
    far0 = lax.ppermute(send0, "xh", SWAP)

    part = pl.pallas_call(
        gram,
        grid_spec=pltpu.PrefetchScalarGridSpec(
            num_scalar_prefetch=1,
            grid=(STEPS,),
            in_specs=[
                pl.BlockSpec((1, 2 * rank, quarter), lambda i, s: (i, 0, 0)),
                pl.BlockSpec((1, quarter, rank), lambda i, s: (1 - s[0], i, 0)),
            ],
            out_specs=pl.BlockSpec((reducers, 2, piece, rank), lambda i, s: (0, 0, 0, 0)),
            scratch_shapes=[pltpu.VMEM((2 * rank, rank), F32)],
        ),
        out_shape=jax.ShapeDtypeStruct((reducers, 2, piece, rank), BF),
        compiler_params=PARAMS,
        name="gram",
    )(pos, left, met)
    part, send1, own_t = lax.optimization_barrier((part, send1, tridiag))
    got = exchange(part, REDUCE)
    far1 = lax.ppermute(send1, "xh", SWAP)
    met_t = exchange(own_t, "xh")

    some = pl.pallas_call(
        add_up,
        out_shape=jax.ShapeDtypeStruct((ring, 2, piece, rank), BF),
        compiler_params=PARAMS,
        name="add_up",
    )(got)
    some, send2 = lax.optimization_barrier((some, send2))
    got = exchange(some, RING)
    far2 = lax.ppermute(send2, "xh", SWAP)

    total = pl.pallas_call(
        add_up_through,
        grid_spec=pltpu.PrefetchScalarGridSpec(
            num_scalar_prefetch=1,
            grid=(1,),
            in_specs=[
                pl.BlockSpec((ring, 2, piece, rank), lambda i, s: (0, 0, 0, 0)),
                pl.BlockSpec((1, rank, rank), lambda i, s: (1 - s[0], 0, 0)),
            ],
            out_specs=pl.BlockSpec((spread, 2, piece, rank), lambda i, s: (0, 0, 0, 0)),
        ),
        out_shape=jax.ShapeDtypeStruct((spread, 2, piece, rank), BF),
        compiler_params=PARAMS,
        name="add_up_through",
    )(pos, got, met_t)
    mats = exchange(total, SPREAD).reshape(2, reducers, 2, piece, rank)

    return pl.pallas_call(
        finish,
        grid_spec=pltpu.PrefetchScalarGridSpec(
            num_scalar_prefetch=1,
            grid=(STEPS,),
            in_specs=[
                pl.BlockSpec((2, reducers, 2, piece, rank), lambda i, s: (0, 0, 0, 0, 0)),
                pl.BlockSpec((1, quarter, rank), lambda i, s: (1 - s[0], i, 0)),
                pl.BlockSpec((quarter, rank), lambda i, s: (0, 0)),
                pl.BlockSpec((quarter, rank), lambda i, s: (0, 0)),
                pl.BlockSpec((quarter, rank), lambda i, s: (jnp.maximum(i - 2, 0), 0)),
                pl.BlockSpec((quarter, 128), lambda i, s: (i, 0)),
            ],
            out_specs=pl.BlockSpec((2, quarter, rank), lambda i, s: (0, i, 0)),
        ),
        out_shape=jax.ShapeDtypeStruct((dims, rows, rank), BF),
        compiler_params=PARAMS,
        name="finish",
    )(pos, mats, met, far0, far1, far2, scale)


def solution(mesh):
    pts = mesh.shape["pts"]
    zh = pts // 16
    fine = Mesh(mesh.devices.reshape(2, zh, 2, 4, 2, 2), ("xl", "zh", "z1", "y", "xh", "core"))
    dim = ("xh", "core")
    points = ("xl", "zh", "z1", "y")
    return jax.shard_map(
        per_device,
        mesh=fine,
        in_specs=(P(dim, points, None), P(dim, None, None), P(points), P(None, points)),
        out_specs=P(dim, points, None),
        check_vma=False,
    )
```

time: 695 us -> 129 us (0.19)
  blocking collectives: 622 us -> 42.2 us
  starting transfers between devices: 7.47 us -> 30.1 us
  matrix products: 17.7 us -> 0 us
  waiting for transfers between devices: 45.6 us -> 33.7 us
  Pallas kernels: 0 us -> 9.71 us
  local copies, waits for them, and re-layouts: 0.8 us -> 10.5 us
    psum x1 -> x0, blocking collectives: 622 us -> none  [per_device(): m_total, g_total = lax.psum((m_part, g_part), 'pts')]
    all_to_all x0 -> x2, blocking collectives: none -> 42.2 us  [exchange(): return lax.all_to_all(x, axes, 0, 0, tiled=True)]
    ppermute x2 -> x3, waiting for transfers between devices: 45.6 us -> 15.4 us  [the longest x1 12.6 us: per_device(): far0 = lax.ppermute(send0, 'xh', SWAP)]
    all_to_all x0 -> x3, starting transfers between devices: none -> 19.5 us  [exchange(): return lax.all_to_all(x, axes, 0, 0, tiled=True)]
    all_to_all x0 -> x3, waiting for transfers between devices: none -> 18.3 us  [exchange(): return lax.all_to_all(x, axes, 0, 0, tiled=True)]
    dot_general x6 -> x0, matrix products: 17.7 us -> none  [the longest x1 4.84 us: per_device(): jnp.einsum('dns,drs->dnr', grad_prod, tridiag, preferred_element_type=jnp...]
    unnamed x12 -> x24, local copies, waits for them, and re-layouts: 0.52 us -> 10.5 us
    pallas_call x0 -> x5, Pallas kernels: none -> 9.71 us  [the longest x1 4.23 us: per_device(): pl.pallas_call(finish, grid_spec=pltpu.PrefetchScalarGridSpec(num_scalar_...]
  transfers between devices with their start and end apart: 2 -> 6, of which waited for: 1 -> 4; matrix products, arithmetic and copies ran while one was open for 1% -> 0% of each run, Pallas kernels for 0% -> 2%
where the time goes in v1:
time: 129 us; the launch traced here: 126 us
  blocking collectives  42.2 us (33%)
  waiting for transfers between devices  33.7 us (26%)
  starting transfers between devices  30.1 us (23%)
  local copies, waits for them, and re-layouts  10.5 us (8%)
  Pallas kernels  9.71 us (8%)
    all_to_all x2, blocking collectives, exchange(): return lax.all_to_all(x, axes, 0, 0, tiled=True)  42.2 us
    all_to_all x3, starting transfers between devices, exchange(): return lax.all_to_all(x, axes, 0, 0, tiled=True)  19.5 us
    all_to_all x3, waiting for transfers between devices, exchange(): return lax.all_to_all(x, axes, 0, 0, tiled=True)  18.3 us
    ppermute x1, waiting for transfers between devices, per_device(): far0 = lax.ppermute(send0, 'xh', SWAP)  12.6 us
    unnamed x24, local copies, waits for them, and re-layouts  10.5 us
    pallas_call x1, Pallas kernels, per_device(): pl.pallas_call(finish, grid_spec=pltpu.PrefetchScalarGridSpec(num_scalar_...  4.23 us
    ppermute x1, starting transfers between devices, per_device(): far0 = lax.ppermute(send0, 'xh', SWAP)  4.09 us
    ppermute x1, starting transfers between devices, per_device(): far2 = lax.ppermute(send2, 'xh', SWAP)  3.26 us
  transfers between devices with their start and end apart: 6, of which 4 were waited for; matrix products, arithmetic and copies ran while one was open for 0% of the time, Pallas kernels for 2%

profile of v1, /device:TPU:6, one launch (start us, length us, event | category | flops | bytes accessed | tf_op | source)
XLA Modules:
  0.0 126.3 jit_solution(9944953896770986904)
XLA Ops:
  0.0 5.3 %all-to-all-start = ((bf16[2,2048,256]{2,1,0:T(8,128)(2,1)}), bf16[2,2048,256]{2,1,0:T(8,128)(2,1)S(1)}, u32[]{:S(2)}, u32[]{:S(2)}) async-start(bf16[2,2048,256]{2,1,0:T(8,128)(2,1)} %q.1), calls=%async_computation | async-start | bytes 4194304 | tf_op jit(solution)/shard_map/all_to_all | solution.py:19
  5.4 1.6 %copy-done = bf16[2,2048,256]{2,1,0:T(8,128)(2,1)S(1)} copy-done((bf16[2,2048,256]{2,1,0:T(8,128)(2,1)S(1)}, bf16[2,2048,256]{2,1,0:T(8,128)(2,1)}, u32[]{:S(2)}) %copy-start) | copy-done | bytes 2097176
  7.0 2.0 %prepare.1 = (bf16[4,512,512]{2,1,0:T(8,128)(2,1)S(1)}, bf16[512,256]{1,0:T(8,128)(2,1)S(1)}, bf16[512,256]{1,0:T(8,128)(2,1)S(1)}, bf16[1024,256]{1,0:T(8,128)(2,1)S(1)}, f32[2048,128]{1,0:T(8,128)S(1)}) custom-call(s32[2]{0:T(128)S(1)} %pad_add_fusion.pos, bf16[2,2048,256]{2,1,0:T(8,128)(2,1)S(1)} %copy-done, bf16[2,256,256]{2,1,0:T(8,128)(2,1)} %t.1, ...), custom_call_target="tpu_custom_call" | custom-call | tf_op jit(solution)/shard_map/prepare/pallas_call | solution.py:136
  9.0 1.3 %copy-done.1 = bf16[4,512,512]{2,1,0:T(8,128)(2,1)} copy-done((bf16[4,512,512]{2,1,0:T(8,128)(2,1)}, bf16[4,512,512]{2,1,0:T(8,128)(2,1)S(1)}, u32[]{:S(2)}) %copy-start.1) | copy-done | bytes 2097176
  10.3 1.0 copy-done.3
  11.3 0.8 copy-done.9
  12.8 0.7 copy-done.11
  13.5 15.2 %all-to-all-done.q.q_near = bf16[2,2048,256]{2,1,0:T(8,128)(2,1)S(1)} async-done(((bf16[2,2048,256]{2,1,0:T(8,128)(2,1)}), bf16[2,2048,256]{2,1,0:T(8,128)(2,1)S(1)}, u32[]{:S(2)}, u32[]{:S(2)}) %all-to-all-start) | async-done | bytes 2097184 | tf_op jit(solution)/shard_map/all_to_all | solution.py:19
  28.7 1.6 %copy-done.2 = bf16[4,512,512]{2,1,0:T(8,128)(2,1)S(1)} copy-done((bf16[4,512,512]{2,1,0:T(8,128)(2,1)S(1)}, bf16[4,512,512]{2,1,0:T(8,128)(2,1)}, u32[]{:S(2)}) %copy-start.2) | copy-done | bytes 2097176
  30.3 1.9 %gram.1 = bf16[16,2,16,256]{3,2,1,0:T(8,128)(2,1)S(1)} custom-call(s32[2]{0:T(128)S(1)} %pad_add_fusion.pos, bf16[4,512,512]{2,1,0:T(8,128)(2,1)S(1)} %copy-done.2, bf16[2,2048,256]{2,1,0:T(8,128)(2,1)S(1)} %all-to-all-done.q.q_near), custom_call_target="tpu_custom_call" | custom-call | tf_op jit(solution)/shard_map/gram/pallas_call | solution.py:167
  32.1 13.6 %all_to_all.25.x = bf16[16,2,16,256]{3,2,1,0:T(8,128)(2,1)S(1)} all-to-all(bf16[16,2,16,256]{3,2,1,0:T(8,128)(2,1)S(1)} %gram.1), channel_id=1, replica_groups=mesh['xl'=2,'zh'=8,'z1'=2,'y'=4,'xh'=2,'core'=2] {'z1','xl','y'}, dimensions={0} | all-to-all | bytes 524288 | tf_op jit(solution)/shard_map/all_to_all | solution.py:19
  45.8 6.7 %all-to-all-start.3 = ((bf16[2,256,256]{2,1,0:T(8,128)(2,1)}), bf16[2,256,256]{2,1,0:T(8,128)(2,1)S(1)}, u32[]{:S(2)}, u32[]{:S(2)}) async-start(bf16[2,256,256]{2,1,0:T(8,128)(2,1)} %t.1), calls=%async_computation.3 | async-start | bytes 524288 | tf_op jit(solution)/shard_map/all_to_all | solution.py:19
  52.5 3.1 %all-to-all-done.3.t = bf16[2,256,256]{2,1,0:T(8,128)(2,1)S(1)} async-done(((bf16[2,256,256]{2,1,0:T(8,128)(2,1)}), bf16[2,256,256]{2,1,0:T(8,128)(2,1)S(1)}, u32[]{:S(2)}, u32[]{:S(2)}) %all-to-all-start.3) | async-done | bytes 262176 | tf_op jit(solution)/shard_map/all_to_all | solution.py:19
  55.6 28.5 %all_to_all.26.x = bf16[8,2,16,256]{3,2,1,0:T(8,128)(2,1)S(1)} all-to-all(bf16[8,2,16,256]{3,2,1,0:T(8,128)(2,1)S(1)} %add_up.1), channel_id=1, replica_groups=mesh['xl'=2,'zh'=8,'z1'=2,'y'=4,'xh'=2,'core'=2] {'zh'}, dimensions={0} | all-to-all | bytes 262144 | tf_op jit(solution)/shard_map/all_to_all | solution.py:19
  84.1 1.5 %add_up_through.1 = bf16[32,2,16,256]{3,2,1,0:T(8,128)(2,1)} custom-call(s32[2]{0:T(128)S(1)} %pad_add_fusion.pos, bf16[8,2,16,256]{3,2,1,0:T(8,128)(2,1)S(1)} %all_to_all.26.x, bf16[2,256,256]{2,1,0:T(8,128)(2,1)S(1)} %all-to-all-done.3.t), custom_call_target="tpu_custom_call" | custom-call | tf_op jit(solution)/shard_map/add_up_through/pallas_call | solution.py:198
  85.7 7.5 %all-to-all-start.4 = ((bf16[32,2,16,256]{3,2,1,0:T(8,128)(2,1)}), bf16[32,2,16,256]{3,2,1,0:T(8,128)(2,1)S(1)}, u32[]{:S(2)}, u32[]{:S(2)}) async-start(bf16[32,2,16,256]{3,2,1,0:T(8,128)(2,1)} %add_up_through.1), calls=%async_computation.4 | async-start | bytes 1048576 | tf_op jit(solution)/shard_map/all_to_all | solution.py:19
  93.2 3.3 %collective-permute-start.2 = (bf16[1024,256]{1,0:T(8,128)(2,1)}, bf16[1024,256]{1,0:T(8,128)(2,1)S(1)}, u32[]{:S(2)}, u32[]{:S(2)}) collective-permute-start(bf16[1024,256]{1,0:T(8,128)(2,1)} %copy-done.9), channel_id=1, source_target_pairs={{0,2},{2,0},{1,3},{3,1},{4,6},{6,4},{5,7},{7,5},{8,10},{10,8},{9,1... | collective-permute-start | bytes 1572872 | tf_op jit(solution)/shard_map/ppermute | solution.py:196
  96.5 4.1 %collective-permute-start = (bf16[512,256]{1,0:T(8,128)(2,1)}, bf16[512,256]{1,0:T(8,128)(2,1)S(1)}, u32[]{:S(2)}, u32[]{:S(2)}) collective-permute-start(bf16[512,256]{1,0:T(8,128)(2,1)} %copy-done.11), channel_id=1, source_target_pairs={{0,2},{2,0},{1,3},{3,1},{4,6},{6,4},{5,7},{7,5},{8,10},{10,8},{9,1... | collective-permute-start | bytes 786440 | tf_op jit(solution)/shard_map/ppermute | solution.py:165
  100.6 3.3 %collective-permute-start.1 = (bf16[512,256]{1,0:T(8,128)(2,1)}, bf16[512,256]{1,0:T(8,128)(2,1)S(1)}, u32[]{:S(2)}, u32[]{:S(2)}) collective-permute-start(bf16[512,256]{1,0:T(8,128)(2,1)} %copy-done.10), channel_id=1, source_target_pairs={{0,2},{2,0},{1,3},{3,1},{4,6},{6,4},{5,7},{7,5},{8,10},{10,8},{9,1... | collective-permute-start | bytes 786440 | tf_op jit(solution)/shard_map/ppermute | solution.py:185
  103.8 12.6 %collective-permute-done.q_far0 = bf16[512,256]{1,0:T(8,128)(2,1)S(1)} collective-permute-done((bf16[512,256]{1,0:T(8,128)(2,1)}, bf16[512,256]{1,0:T(8,128)(2,1)S(1)}, u32[]{:S(2)}, u32[]{:S(2)}) %collective-permute-start) | collective-permute-done | bytes 262176 | tf_op jit(solution)/shard_map/ppermute | solution.py:165
  116.4 2.8 %collective-permute-done.1.q_far1 = bf16[512,256]{1,0:T(8,128)(2,1)S(1)} collective-permute-done((bf16[512,256]{1,0:T(8,128)(2,1)}, bf16[512,256]{1,0:T(8,128)(2,1)S(1)}, u32[]{:S(2)}, u32[]{:S(2)}) %collective-permute-start.1) | collective-permute-done | bytes 262176 | tf_op jit(solution)/shard_map/ppermute | solution.py:185
  119.9 1.2 copy-done.4
  121.2 0.9 copy-done.6
  122.1 4.2 %finish.1 = bf16[2,2048,256]{2,1,0:T(8,128)(2,1)} custom-call(s32[2]{0:T(128)S(1)} %pad_add_fusion.pos, bf16[2,16,2,16,256]{4,3,2,1,0:T(8,128)(2,1)S(1)} %bitcast.4, bf16[2,2048,256]{2,1,0:T(8,128)(2,1)S(1)} %all-to-all-done.q.q_near, bf16[512,256]{1,0:T(8,128)(2,1)S(1)} %collective-permute-done.q_far0, bf16[512,256]{1,0:T(8,128)(2,1)S(1)} %copy-done.6, ...), custom_call_target="tpu_custom_call" | custom-call | tf_op jit(solution)/shard_map/finish/pallas_call | solution.py:215
  (20 shorter events, 1.5 us)
Async XLA Ops:
  0.0 5.4 %copy-start.7 = (f32[4,2048]{1,0:T(4,128)S(1)}, f32[4,2048]{1,0:T(4,128)}, u32[]{:S(2)}) copy-start(f32[4,2048]{1,0:T(4,128)} %c.1) | copy-start | bytes 98308
  0.0 5.4 %copy-start.8 = (f32[2048]{0:T(1024)S(1)}, f32[2048]{0:T(1024)}, u32[]{:S(2)}) copy-start(f32[2048]{0:T(1024)} %param.6) | copy-start | bytes 24580
  0.0 28.7 %all-to-all-start = ((bf16[2,2048,256]{2,1,0:T(8,128)(2,1)}), bf16[2,2048,256]{2,1,0:T(8,128)(2,1)S(1)}, u32[]{:S(2)}, u32[]{:S(2)}) async-start(bf16[2,2048,256]{2,1,0:T(8,128)(2,1)} %q.1), calls=%async_computation | async-start | bytes 4194304 | tf_op jit(solution)/shard_map/all_to_all | solution.py:19
  5.4 1.6 %copy-start = (bf16[2,2048,256]{2,1,0:T(8,128)(2,1)S(1)}, bf16[2,2048,256]{2,1,0:T(8,128)(2,1)}, u32[]{:S(2)}) copy-start(bf16[2,2048,256]{2,1,0:T(8,128)(2,1)} %q.1) | copy-start | bytes 6291460
  9.0 1.3 %copy-start.1 = (bf16[4,512,512]{2,1,0:T(8,128)(2,1)}, bf16[4,512,512]{2,1,0:T(8,128)(2,1)S(1)}, u32[]{:S(2)}) copy-start(bf16[4,512,512]{2,1,0:T(8,128)(2,1)S(1)} %get-tuple-element.15.left) | copy-start | bytes 6291460
  10.3 1.0 copy-start.3
  11.3 0.8 copy-start.9
  12.1 0.7 copy-start.10
  12.8 0.7 copy-start.11
  28.7 1.6 %copy-start.2 = (bf16[4,512,512]{2,1,0:T(8,128)(2,1)S(1)}, bf16[4,512,512]{2,1,0:T(8,128)(2,1)}, u32[]{:S(2)}) copy-start(bf16[4,512,512]{2,1,0:T(8,128)(2,1)} %copy-done.1) | copy-start | bytes 6291460
  45.8 9.8 %all-to-all-start.3 = ((bf16[2,256,256]{2,1,0:T(8,128)(2,1)}), bf16[2,256,256]{2,1,0:T(8,128)(2,1)S(1)}, u32[]{:S(2)}, u32[]{:S(2)}) async-start(bf16[2,256,256]{2,1,0:T(8,128)(2,1)} %t.1), calls=%async_computation.3 | async-start | bytes 524288 | tf_op jit(solution)/shard_map/all_to_all | solution.py:19
  85.7 34.3 %all-to-all-start.4 = ((bf16[32,2,16,256]{3,2,1,0:T(8,128)(2,1)}), bf16[32,2,16,256]{3,2,1,0:T(8,128)(2,1)S(1)}, u32[]{:S(2)}, u32[]{:S(2)}) async-start(bf16[32,2,16,256]{3,2,1,0:T(8,128)(2,1)} %add_up_through.1), calls=%async_computation.4 | async-start | bytes 1048576 | tf_op jit(solution)/shard_map/all_to_all | solution.py:19
  93.2 26.7 %collective-permute-start.2 = (bf16[1024,256]{1,0:T(8,128)(2,1)}, bf16[1024,256]{1,0:T(8,128)(2,1)S(1)}, u32[]{:S(2)}, u32[]{:S(2)}) collective-permute-start(bf16[1024,256]{1,0:T(8,128)(2,1)} %copy-done.9), channel_id=1, source_target_pairs={{0,2},{2,0},{1,3},{3,1},{4,6},{6,4},{5,7},{7,5},{8,10},{10,8},{9,1... | collective-permute-start | bytes 1572872 | tf_op jit(solution)/shard_map/ppermute | solution.py:196
  96.5 20.0 %collective-permute-start = (bf16[512,256]{1,0:T(8,128)(2,1)}, bf16[512,256]{1,0:T(8,128)(2,1)S(1)}, u32[]{:S(2)}, u32[]{:S(2)}) collective-permute-start(bf16[512,256]{1,0:T(8,128)(2,1)} %copy-done.11), channel_id=1, source_target_pairs={{0,2},{2,0},{1,3},{3,1},{4,6},{6,4},{5,7},{7,5},{8,10},{10,8},{9,1... | collective-permute-start | bytes 786440 | tf_op jit(solution)/shard_map/ppermute | solution.py:165
  100.6 18.7 %collective-permute-start.1 = (bf16[512,256]{1,0:T(8,128)(2,1)}, bf16[512,256]{1,0:T(8,128)(2,1)S(1)}, u32[]{:S(2)}, u32[]{:S(2)}) collective-permute-start(bf16[512,256]{1,0:T(8,128)(2,1)} %copy-done.10), channel_id=1, source_target_pairs={{0,2},{2,0},{1,3},{3,1},{4,6},{6,4},{5,7},{7,5},{8,10},{10,8},{9,1... | collective-permute-start | bytes 786440 | tf_op jit(solution)/shard_map/ppermute | solution.py:185
  119.2 0.7 copy-start.5
  119.9 1.2 copy-start.4
  121.2 0.9 copy-start.6

commit v2 on v1

v2 whole, which is shorter than its diff:
```python
import jax
import jax.numpy as jnp
from jax import lax
from jax.experimental import pallas as pl
from jax.experimental.pallas import tpu as pltpu
from jax.sharding import Mesh, PartitionSpec as P

BF = jnp.bfloat16
F32 = jnp.float32
PARAMS = pltpu.CompilerParams(vmem_limit_bytes=24 * 1024 * 1024)
SWAP = [(0, 1), (1, 0)]
REDUCE = ("z1", "xl", "y")
RING = "zh"
SPREAD = ("xh", "z1", "xl", "y")
STEPS = 4
ANY = pl.BlockSpec(memory_space=pl.ANY)
HBM = pl.BlockSpec(memory_space=pltpu.HBM)
SMEM = pl.BlockSpec(memory_space=pltpu.SMEM)
VMEM = pl.BlockSpec(memory_space=pltpu.VMEM)


def like(x):
    return jax.ShapeDtypeStruct(x.shape, x.dtype)


def exchange(x, axes):
    return lax.all_to_all(x, axes, 0, 0, tiled=True)


def prepare(pos, q, t, v, c, prod, weights, send, scale, bands):
    step = pl.program_id(0)
    q_own = q[0]
    rows, rank = q_own.shape

    @pl.when(step == 0)
    def _():
        row = lax.broadcasted_iota(jnp.int32, (rank, rank), 0)
        column = lax.broadcasted_iota(jnp.int32, (rank, rank), 1)
        line = lax.broadcasted_iota(jnp.int32, bands.shape, 0)
        full = t[1 - pos[0]].astype(F32)
        band = jnp.zeros(bands.shape, F32)
        for k in range(3):
            entries = jnp.sum(jnp.where(row == column + (k - 1), full, 0.0), axis=0, keepdims=True)
            band = jnp.where(line == k, entries, band)
        bands[...] = band.astype(BF)

    send[...] = q_own
    own = lax.dot_general(t[pos[0]], q_own, (((1,), (1,)), ((), ())), preferred_element_type=F32)
    prod[0] = own.astype(BF)
    c_near = c[pl.ds(pos[1] * 2 + pos[0], 1), :]
    c_far = c[pl.ds(pos[1] * 2 + 1 - pos[0], 1), :]
    line = lax.broadcasted_iota(jnp.int32, weights.shape[1:], 0)
    weights[0] = jnp.where(line == 0, v[...], c_near)
    row = lax.broadcasted_iota(jnp.int32, (128, rows), 0)
    scale[...] = jnp.where(row == 0, v[...], jnp.where(row == 1, c_near, c_far)).T


def gram(pos, prod, weights, q, bands, send, out, sent, prod_here, weights_here, sems):
    del bands, send, sent
    parts, kinds, rows, rank = out.shape
    copies = [pltpu.make_async_copy(weights, weights_here, sems.at[STEPS])]
    copies += [pltpu.make_async_copy(prod.at[k], prod_here.at[k], sems.at[k]) for k in range(STEPS)]
    for copy in copies:
        copy.start()
    copies[0].wait()
    left = []
    for k in range(STEPS):
        copies[k + 1].wait()
        block = prod_here[k].astype(F32)
        left.append(jnp.concatenate([(block * weights_here[k, n : n + 1]).astype(BF) for n in range(kinds)], axis=0))
    total = jnp.dot(jnp.concatenate(left, axis=1), q[1 - pos[0]], preferred_element_type=F32)
    total = total.astype(BF)
    for kind in range(kinds):
        for part in range(parts):
            at = kind * rank + part * rows
            out[part, kind] = total[at : at + rows]


def total_of(x):
    total = x[0].astype(F32)
    for k in range(1, x.shape[0]):
        total = total + x[k].astype(F32)
    return total


def add_up(x, out):
    total = total_of(x).astype(BF)
    for k in range(out.shape[0]):
        out[k] = total


def add_up_through(x, bands, far, out):
    del far
    total = total_of(x)
    kinds, rows, rank = total.shape
    flat = total.reshape(kinds * rows, rank)
    band = bands[...].astype(F32)
    res = flat * band[1:2] + pltpu.roll(flat, 1, 1) * band[0:1] + pltpu.roll(flat, rank - 1, 1) * band[2:3]
    res = res.astype(BF).reshape(kinds, rows, rank)
    for k in range(out.shape[0]):
        out[k] = res


def finish(pos, mats, q_near, q_far, scale, out, here, sems):
    near = pos[0]
    slots, parts, kinds, rows, rank = mats.shape
    width = here.shape[2]

    def pick(slot, kind):
        return mats[slot, :, kind].reshape(parts * rows, rank)

    def across(q, m):
        return lax.dot_general(q, m, (((1,), (1,)), ((), ())), preferred_element_type=F32)

    def straight(q, m):
        return jnp.dot(q, m, preferred_element_type=F32)

    copies = []
    for which, slot, multiply in ((0, near, across), (1, 1 - near, straight)):
        by_c = pick(slot, 0)
        by_v = pick(slot, 1)
        for k in range(STEPS):
            span = pl.ds(k * width, width)
            q = q_near[1 - near, span] if which == 0 else q_far[span]
            res = scale[span, 1 + which : 2 + which] * multiply(q, by_c) + scale[span, 0:1] * multiply(q, by_v)
            here[which, k] = res.astype(BF)
            copy = pltpu.make_async_copy(here.at[which, k], out.at[slot, span], sems.at[which, k])
            copy.start()
            copies.append(copy)
    for copy in copies:
        copy.wait()


def per_device(factors, tridiag, probe_vector, cotangent):
    dims, rows, rank = factors.shape
    quarter = rows // STEPS
    reducers = lax.axis_size(REDUCE)
    ring = lax.axis_size(RING)
    spread = lax.axis_size(SPREAD)
    piece = rank // reducers
    pos = jnp.stack([lax.axis_index("xh"), lax.axis_index("core")]).astype(jnp.int32)
    v = probe_vector.reshape(1, rows)

    met = exchange(factors, "xh")
    prod, weights, send, scale, bands = pl.pallas_call(
        prepare,
        grid_spec=pltpu.PrefetchScalarGridSpec(
            num_scalar_prefetch=1,
            grid=(STEPS,),
            in_specs=[
                pl.BlockSpec((1, quarter, rank), lambda i, s: (s[0], i, 0)),
                pl.BlockSpec((dims, rank, rank), lambda i, s: (0, 0, 0)),
                pl.BlockSpec((1, quarter), lambda i, s: (0, i)),
                pl.BlockSpec((cotangent.shape[0], quarter), lambda i, s: (0, i)),
            ],
            out_specs=[
                pl.BlockSpec((1, rank, quarter), lambda i, s: (i, 0, 0)),
                pl.BlockSpec((1, 8, quarter), lambda i, s: (i, 0, 0)),
                pl.BlockSpec((quarter, rank), lambda i, s: (i, 0)),
                pl.BlockSpec((quarter, 128), lambda i, s: (i, 0)),
                pl.BlockSpec((16, rank), lambda i, s: (0, 0)),
            ],
        ),
        out_shape=[
            jax.ShapeDtypeStruct((STEPS, rank, quarter), BF),
            jax.ShapeDtypeStruct((STEPS, 8, quarter), F32),
            jax.ShapeDtypeStruct((rows, rank), BF),
            jax.ShapeDtypeStruct((rows, 128), F32),
            jax.ShapeDtypeStruct((16, rank), BF),
        ],
        compiler_params=PARAMS,
        name="prepare",
    )(pos, factors, tridiag, v, cotangent)
    bands = lax.ppermute(bands, "xh", SWAP)

    part, send = pl.pallas_call(
        gram,
        in_specs=[SMEM, HBM, HBM, VMEM, ANY, ANY],
        out_specs=[VMEM, ANY],
        out_shape=[jax.ShapeDtypeStruct((reducers, 2, piece, rank), BF), like(send)],
        scratch_shapes=[
            pltpu.VMEM(prod.shape, BF),
            pltpu.VMEM(weights.shape, F32),
            pltpu.SemaphoreType.DMA((STEPS + 1,)),
        ],
        input_output_aliases={5: 1},
        compiler_params=PARAMS,
        name="gram",
    )(pos, prod, weights, met, bands, send)
    got = exchange(part, REDUCE)
    far = lax.ppermute(send, "xh", SWAP)

    some = pl.pallas_call(
        add_up,
        in_specs=[VMEM],
        out_specs=VMEM,
        out_shape=jax.ShapeDtypeStruct((ring, 2, piece, rank), BF),
        compiler_params=PARAMS,
        name="add_up",
    )(got)
    got = exchange(some, RING)

    total = pl.pallas_call(
        add_up_through,
        in_specs=[VMEM, VMEM, ANY],
        out_specs=VMEM,
        out_shape=jax.ShapeDtypeStruct((spread, 2, piece, rank), BF),
        compiler_params=PARAMS,
        name="add_up_through",
    )(got, bands, far)
    mats = exchange(total, SPREAD).reshape(2, reducers, 2, piece, rank)

    return pl.pallas_call(
        finish,
        in_specs=[SMEM, VMEM, VMEM, VMEM, VMEM],
        out_specs=HBM,
        out_shape=jax.ShapeDtypeStruct((dims, rows, rank), BF),
        scratch_shapes=[pltpu.VMEM((2, STEPS, quarter, rank), BF), pltpu.SemaphoreType.DMA((2, STEPS))],
        compiler_params=PARAMS,
        name="finish",
    )(pos, mats, met, far, scale)


def solution(mesh):
    pts = mesh.shape["pts"]
    zh = pts // 16
    fine = Mesh(mesh.devices.reshape(2, zh, 2, 4, 2, 2), ("xl", "zh", "z1", "y", "xh", "core"))
    dim = ("xh", "core")
    points = ("xl", "zh", "z1", "y")
    return jax.shard_map(
        per_device,
        mesh=fine,
        in_specs=(P(dim, points, None), P(dim, None, None), P(points), P(None, points)),
        out_specs=P(dim, points, None),
        check_vma=False,
    )
```

time: 129 us -> 96.1 us (0.74); the launches traced: 126 us -> 94.9 us
  blocking collectives: 42.2 us -> 15.4 us
  local copies, waits for them, and re-layouts: 10.5 us -> 6.45 us
  starting transfers between devices: 30.1 us -> 33.8 us
  Pallas kernels: 9.71 us -> 7.23 us
  waiting for transfers between devices: 33.7 us -> 31.8 us
    all_to_all x2 -> x1, blocking collectives: 42.2 us -> 15.4 us  [exchange(): return lax.all_to_all(x, axes, 0, 0, tiled=True)]
    all_to_all x3, waiting for transfers between devices: 18.3 us -> 8.45 us  [exchange(): return lax.all_to_all(x, axes, 0, 0, tiled=True)]
    ppermute x3 -> x2, waiting for transfers between devices: 15.4 us -> 23.4 us  [the longest x1 16.1 us: per_device(): bands = lax.ppermute(bands, 'xh', SWAP)]
    all_to_all x3, starting transfers between devices: 19.5 us -> 26.8 us  [exchange(): return lax.all_to_all(x, axes, 0, 0, tiled=True)]
    unnamed x24 -> x20, local copies, waits for them, and re-layouts: 10.5 us -> 6.45 us
    ppermute x3 -> x2, starting transfers between devices: 10.6 us -> 7.05 us  [the longest x1 5.13 us: per_device(): far = lax.ppermute(send, 'xh', SWAP)]
    pallas_call x4, Pallas kernels: 7.67 us -> 5.36 us  [the longest x1 2.74 us: per_device(): pl.pallas_call(finish, in_specs=[SMEM, VMEM, VMEM, VMEM, VMEM], out_specs...]
  transfers between devices with their start and end apart: 6 -> 5, of which waited for: 4 -> 4; matrix products, arithmetic and copies ran while one was open for 0% -> 0% of each run, Pallas kernels for 2% -> 3%
where the time goes in v2:
time: 96.1 us; the launch traced here: 94.9 us
  starting transfers between devices  33.8 us (35%)
  waiting for transfers between devices  31.8 us (33%)
  blocking collectives  15.4 us (16%)
  Pallas kernels  7.23 us (8%)
  local copies, waits for them, and re-layouts  6.45 us (7%)
    all_to_all x3, starting transfers between devices, exchange(): return lax.all_to_all(x, axes, 0, 0, tiled=True)  26.8 us
    ppermute x1, waiting for transfers between devices, per_device(): bands = lax.ppermute(bands, 'xh', SWAP)  16.1 us
    all_to_all x1, blocking collectives, exchange(): return lax.all_to_all(x, axes, 0, 0, tiled=True)  15.4 us
    all_to_all x3, waiting for transfers between devices, exchange(): return lax.all_to_all(x, axes, 0, 0, tiled=True)  8.45 us
    ppermute x1, waiting for transfers between devices, per_device(): far = lax.ppermute(send, 'xh', SWAP)  7.24 us
    unnamed x20, local copies, waits for them, and re-layouts  6.45 us
    ppermute x1, starting transfers between devices, per_device(): far = lax.ppermute(send, 'xh', SWAP)  5.13 us
    pallas_call x1, Pallas kernels, per_device(): pl.pallas_call(finish, in_specs=[SMEM, VMEM, VMEM, VMEM, VMEM], out_specs...  2.74 us
  transfers between devices with their start and end apart: 5, of which 4 were waited for; matrix products, arithmetic and copies ran while one was open for 0% of the time, Pallas kernels for 3%

profile of v2, /device:TPU:6, one launch (start us, length us, event | category | flops | bytes accessed | tf_op | source)
XLA Modules:
  0.0 94.9 jit_solution(17654756160555101143)
XLA Ops:
  0.0 5.3 %all-to-all-start = ((bf16[2,2048,256]{2,1,0:T(8,128)(2,1)}), bf16[2,2048,256]{2,1,0:T(8,128)(2,1)S(1)}, u32[]{:S(2)}, u32[]{:S(2)}) async-start(bf16[2,2048,256]{2,1,0:T(8,128)(2,1)} %q.1), calls=%async_computation | async-start | bytes 4194304 | tf_op jit(solution)/shard_map/all_to_all | solution.py:27
  5.3 0.1 pad_add_fusion.pos
  5.4 1.6 %copy-done = bf16[2,2048,256]{2,1,0:T(8,128)(2,1)S(1)} copy-done((bf16[2,2048,256]{2,1,0:T(8,128)(2,1)S(1)}, bf16[2,2048,256]{2,1,0:T(8,128)(2,1)}, u32[]{:S(2)}) %copy-start) | copy-done | bytes 2097176
  7.0 1.9 %prepare.1 = (bf16[4,256,512]{2,1,0:T(8,128)(2,1)S(1)}, f32[4,8,512]{2,1,0:T(8,128)S(1)}, bf16[2048,256]{1,0:T(8,128)(2,1)S(1)}, f32[2048,128]{1,0:T(8,128)S(1)}, bf16[16,256]{1,0:T(8,128)(2,1)S(1)}) custom-call(s32[2]{0:T(128)S(1)} %pad_add_fusion.pos, bf16[2,2048,256]{2,1,0:T(8,128)(2,1)S(1)} %copy-done, bf16[2,256,256]{2,1,0:T(8,128)(2,1)S(1)} %copy-done.7, ...), custom_call_target="tpu_custom_call" | custom-call | tf_op jit(solution)/shard_map/prepare/pallas_call | solution.py:145
  8.9 0.0 copy-start.1
  8.9 1.0 %copy-done.1 = bf16[2048,256]{1,0:T(8,128)(2,1)} copy-done((bf16[2048,256]{1,0:T(8,128)(2,1)}, bf16[2048,256]{1,0:T(8,128)(2,1)S(1)}, u32[]{:S(2)}) %copy-start.1) | copy-done | bytes 1048600
  9.8 1.0 %copy-done.4 = f32[2048,128]{1,0:T(8,128)} copy-done((f32[2048,128]{1,0:T(8,128)}, f32[2048,128]{1,0:T(8,128)S(1)}, u32[]{:S(2)}) %copy-start.4) | copy-done | bytes 1048600
  10.8 1.9 %collective-permute-start = (bf16[16,256]{1,0:T(8,128)(2,1)S(1)}, bf16[16,256]{1,0:T(8,128)(2,1)S(1)}, u32[]{:S(2)}, u32[]{:S(2)}) collective-permute-start(bf16[16,256]{1,0:T(8,128)(2,1)S(1)} %get-tuple-element.14), channel_id=1, source_target_pairs={{0,2},{2,0},{1,3},{3,1},{4,6},{6,4},{5,7},{7,5},{8,10},{10,8},{9,1... | collective-permute-start | bytes 24584 | tf_op jit(solution)/shard_map/ppermute | solution.py:174
  12.7 16.1 %collective-permute-done.bands = bf16[16,256]{1,0:T(8,128)(2,1)S(1)} collective-permute-done((bf16[16,256]{1,0:T(8,128)(2,1)S(1)}, bf16[16,256]{1,0:T(8,128)(2,1)S(1)}, u32[]{:S(2)}, u32[]{:S(2)}) %collective-permute-start) | collective-permute-done | bytes 8224 | tf_op jit(solution)/shard_map/ppermute | solution.py:174
  28.9 1.2 %copy-done.2 = bf16[2048,256]{1,0:T(8,128)(2,1)S(1)} copy-done((bf16[2048,256]{1,0:T(8,128)(2,1)S(1)}, bf16[2048,256]{1,0:T(8,128)(2,1)}, u32[]{:S(2)}) %copy-start.2) | copy-done | bytes 1048600
  30.1 1.8 %gram.1 = (bf16[16,2,16,256]{3,2,1,0:T(8,128)(2,1)S(1)}, bf16[2048,256]{1,0:T(8,128)(2,1)S(1)}) custom-call(s32[2]{0:T(128)S(1)} %pad_add_fusion.pos, bf16[4,256,512]{2,1,0:T(8,128)(2,1)S(1)} %get-tuple-element.12.prod, f32[4,8,512]{2,1,0:T(8,128)S(1)} %get-tuple-element.13.weights, ...), custom_call_target="tpu_custom_call", output_to_operand_aliasing={{1}: (5, {})} | custom-call | tf_op jit(solution)/shard_map/gram/pallas_call | solution.py:176
  31.9 0.0 copy-start.3
  31.9 1.0 %copy-done.3 = bf16[2048,256]{1,0:T(8,128)(2,1)} copy-done((bf16[2048,256]{1,0:T(8,128)(2,1)}, bf16[2048,256]{1,0:T(8,128)(2,1)S(1)}, u32[]{:S(2)}) %copy-start.3) | copy-done | bytes 1048600
  32.9 0.7 copy-done.6
  33.6 7.3 %all-to-all-start.1 = ((bf16[16,2,16,256]{3,2,1,0:T(8,128)(2,1)}), bf16[16,2,16,256]{3,2,1,0:T(8,128)(2,1)S(1)}, u32[]{:S(2)}, u32[]{:S(2)}) async-start(bf16[16,2,16,256]{3,2,1,0:T(8,128)(2,1)} %copy-done.6), calls=%async_computation.1 | async-start | bytes 524288 | tf_op jit(solution)/shard_map/all_to_all | solution.py:27
  40.9 5.1 %collective-permute-start.1 = (bf16[2048,256]{1,0:T(8,128)(2,1)}, bf16[2048,256]{1,0:T(8,128)(2,1)S(1)}, u32[]{:S(2)}, u32[]{:S(2)}) collective-permute-start(bf16[2048,256]{1,0:T(8,128)(2,1)} %copy-done.3), channel_id=1, source_target_pairs={{0,2},{2,0},{1,3},{3,1},{4,6},{6,4},{5,7},{7,5},{8,10},{10,8},{9,1... | collective-permute-start | bytes 3145736 | tf_op jit(solution)/shard_map/ppermute | solution.py:191
  46.0 1.5 %all-to-all-done.1.x = bf16[16,2,16,256]{3,2,1,0:T(8,128)(2,1)S(1)} async-done(((bf16[16,2,16,256]{3,2,1,0:T(8,128)(2,1)}), bf16[16,2,16,256]{3,2,1,0:T(8,128)(2,1)S(1)}, u32[]{:S(2)}, u32[]{:S(2)}) %all-to-all-start.1) | async-done | bytes 262176 | tf_op jit(solution)/shard_map/all_to_all | solution.py:27
  47.5 0.7 add_up.1
  48.2 14.2 %all-to-all-start.2 = ((bf16[8,2,16,256]{3,2,1,0:T(8,128)(2,1)}), bf16[8,2,16,256]{3,2,1,0:T(8,128)(2,1)S(1)}, u32[]{:S(2)}, u32[]{:S(2)}) async-start(bf16[8,2,16,256]{3,2,1,0:T(8,128)(2,1)} %add_up.1), calls=%async_computation.2 | async-start | bytes 262144 | tf_op jit(solution)/shard_map/all_to_all | solution.py:27
  62.4 7.2 %collective-permute-done.1.far.q_far = bf16[2048,256]{1,0:T(8,128)(2,1)S(1)} collective-permute-done((bf16[2048,256]{1,0:T(8,128)(2,1)}, bf16[2048,256]{1,0:T(8,128)(2,1)S(1)}, u32[]{:S(2)}, u32[]{:S(2)}) %collective-permute-start.1) | collective-permute-done | bytes 1048608 | tf_op jit(solution)/shard_map/ppermute | solution.py:191
  69.7 6.9 %all-to-all-done.2.x = bf16[8,2,16,256]{3,2,1,0:T(8,128)(2,1)S(1)} async-done(((bf16[8,2,16,256]{3,2,1,0:T(8,128)(2,1)}), bf16[8,2,16,256]{3,2,1,0:T(8,128)(2,1)S(1)}, u32[]{:S(2)}, u32[]{:S(2)}) %all-to-all-start.2) | async-done | bytes 131104 | tf_op jit(solution)/shard_map/all_to_all | solution.py:27
  76.6 0.1 add_up_through.1
  76.8 15.4 %all_to_all.20 = bf16[32,2,16,256]{3,2,1,0:T(8,128)(2,1)S(1)} all-to-all(bf16[32,2,16,256]{3,2,1,0:T(8,128)(2,1)S(1)} %add_up_through.1), channel_id=1, replica_groups=mesh['xl'=2,'zh'=8,'z1'=2,'y'=4,'xh'=2,'core'=2] {'xh','z1','xl','y'}, dimensions={0} | all-to-all | bytes 1048576 | tf_op jit(solution)/shard_map/all_to_all | solution.py:27
  92.2 2.7 %finish.1 = bf16[2,2048,256]{2,1,0:T(8,128)(2,1)} custom-call(s32[2]{0:T(128)S(1)} %pad_add_fusion.pos, bf16[2,16,2,16,256]{4,3,2,1,0:T(8,128)(2,1)S(1)} %bitcast.4, bf16[2,2048,256]{2,1,0:T(8,128)(2,1)S(1)} %all-to-all-done.q.q_near, bf16[2048,256]{1,0:T(8,128)(2,1)S(1)} %collective-permute-done.1.far.q_far, f32[2048,128]{1,0:T(8,128)S(1)} %copy-done.5), custom_call_target="tpu_custom_call" | custom-call | tf_op jit(solution)/shard_map/finish/pallas_call | solution.py:213
  (13 shorter events, 0.0 us)
Async XLA Ops:
  0.0 5.4 %copy-start.8 = (f32[4,2048]{1,0:T(4,128)S(1)}, f32[4,2048]{1,0:T(4,128)}, u32[]{:S(2)}) copy-start(f32[4,2048]{1,0:T(4,128)} %c.1) | copy-start | bytes 98308
  0.0 5.4 %copy-start.9 = (f32[2048]{0:T(1024)S(1)}, f32[2048]{0:T(1024)}, u32[]{:S(2)}) copy-start(f32[2048]{0:T(1024)} %param.6) | copy-start | bytes 24580
  0.0 5.4 %copy-start.7 = (bf16[2,256,256]{2,1,0:T(8,128)(2,1)S(1)}, bf16[2,256,256]{2,1,0:T(8,128)(2,1)}, u32[]{:S(2)}) copy-start(bf16[2,256,256]{2,1,0:T(8,128)(2,1)} %t.1) | copy-start | bytes 786436
  0.0 28.9 %all-to-all-start = ((bf16[2,2048,256]{2,1,0:T(8,128)(2,1)}), bf16[2,2048,256]{2,1,0:T(8,128)(2,1)S(1)}, u32[]{:S(2)}, u32[]{:S(2)}) async-start(bf16[2,2048,256]{2,1,0:T(8,128)(2,1)} %q.1), calls=%async_computation | async-start | bytes 4194304 | tf_op jit(solution)/shard_map/all_to_all | solution.py:27
  5.4 1.6 %copy-start = (bf16[2,2048,256]{2,1,0:T(8,128)(2,1)S(1)}, bf16[2,2048,256]{2,1,0:T(8,128)(2,1)}, u32[]{:S(2)}) copy-start(bf16[2,2048,256]{2,1,0:T(8,128)(2,1)} %q.1) | copy-start | bytes 6291460
  8.9 1.0 %copy-start.1 = (bf16[2048,256]{1,0:T(8,128)(2,1)}, bf16[2048,256]{1,0:T(8,128)(2,1)S(1)}, u32[]{:S(2)}) copy-start(bf16[2048,256]{1,0:T(8,128)(2,1)S(1)} %get-tuple-element.15.send) | copy-start | bytes 3145732
  9.8 1.0 %copy-start.4 = (f32[2048,128]{1,0:T(8,128)}, f32[2048,128]{1,0:T(8,128)S(1)}, u32[]{:S(2)}) copy-start(f32[2048,128]{1,0:T(8,128)S(1)} %get-tuple-element.18.scale) | copy-start | bytes 3145732
  10.8 18.0 %collective-permute-start = (bf16[16,256]{1,0:T(8,128)(2,1)S(1)}, bf16[16,256]{1,0:T(8,128)(2,1)S(1)}, u32[]{:S(2)}, u32[]{:S(2)}) collective-permute-start(bf16[16,256]{1,0:T(8,128)(2,1)S(1)} %get-tuple-element.14), channel_id=1, source_target_pairs={{0,2},{2,0},{1,3},{3,1},{4,6},{6,4},{5,7},{7,5},{8,10},{10,8},{9,1... | collective-permute-start | bytes 24584 | tf_op jit(solution)/shard_map/ppermute | solution.py:174
  28.9 1.2 %copy-start.2 = (bf16[2048,256]{1,0:T(8,128)(2,1)S(1)}, bf16[2048,256]{1,0:T(8,128)(2,1)}, u32[]{:S(2)}) copy-start(bf16[2048,256]{1,0:T(8,128)(2,1)} %copy-done.1) | copy-start | bytes 3145732
  31.9 1.0 %copy-start.3 = (bf16[2048,256]{1,0:T(8,128)(2,1)}, bf16[2048,256]{1,0:T(8,128)(2,1)S(1)}, u32[]{:S(2)}) copy-start(bf16[2048,256]{1,0:T(8,128)(2,1)S(1)} %get-tuple-element.17) | copy-start | bytes 3145732
  32.9 0.7 copy-start.6
  33.6 14.0 %all-to-all-start.1 = ((bf16[16,2,16,256]{3,2,1,0:T(8,128)(2,1)}), bf16[16,2,16,256]{3,2,1,0:T(8,128)(2,1)S(1)}, u32[]{:S(2)}, u32[]{:S(2)}) async-start(bf16[16,2,16,256]{3,2,1,0:T(8,128)(2,1)} %copy-done.6), calls=%async_computation.1 | async-start | bytes 524288 | tf_op jit(solution)/shard_map/all_to_all | solution.py:27
  40.9 28.8 %collective-permute-start.1 = (bf16[2048,256]{1,0:T(8,128)(2,1)}, bf16[2048,256]{1,0:T(8,128)(2,1)S(1)}, u32[]{:S(2)}, u32[]{:S(2)}) collective-permute-start(bf16[2048,256]{1,0:T(8,128)(2,1)} %copy-done.3), channel_id=1, source_target_pairs={{0,2},{2,0},{1,3},{3,1},{4,6},{6,4},{5,7},{7,5},{8,10},{10,8},{9,1... | collective-permute-start | bytes 3145736 | tf_op jit(solution)/shard_map/ppermute | solution.py:191
  48.2 28.4 %all-to-all-start.2 = ((bf16[8,2,16,256]{3,2,1,0:T(8,128)(2,1)}), bf16[8,2,16,256]{3,2,1,0:T(8,128)(2,1)S(1)}, u32[]{:S(2)}, u32[]{:S(2)}) async-start(bf16[8,2,16,256]{3,2,1,0:T(8,128)(2,1)} %add_up.1), calls=%async_computation.2 | async-start | bytes 262144 | tf_op jit(solution)/shard_map/all_to_all | solution.py:27
  76.6 15.6 %copy-start.5 = (f32[2048,128]{1,0:T(8,128)S(1)}, f32[2048,128]{1,0:T(8,128)}, u32[]{:S(2)}) copy-start(f32[2048,128]{1,0:T(8,128)} %copy-done.4) | copy-start | bytes 3145732

commit v3 on v2

--- a/solution.py
+++ b/solution.py
@@ -23,11 +23,12 @@
     return jax.ShapeDtypeStruct(x.shape, x.dtype)
 
 
-def exchange(x, axes):
-    return lax.all_to_all(x, axes, 0, 0, tiled=True)
-
-
-def prepare(pos, q, t, v, c, prod, weights, send, scale, bands):
+def exchange(x, axes, order=None):
+    groups = None if order is None else [order]
+    return lax.all_to_all(x, axes, 0, 0, tiled=True, axis_index_groups=groups)
+
+
+def prepare(pos, q, t, v, c, prod, weights, send, bands):
     step = pl.program_id(0)
     q_own = q[0]
     rows, rank = q_own.shape
@@ -50,30 +51,25 @@
     c_near = c[pl.ds(pos[1] * 2 + pos[0], 1), :]
     c_far = c[pl.ds(pos[1] * 2 + 1 - pos[0], 1), :]
     line = lax.broadcasted_iota(jnp.int32, weights.shape[1:], 0)
-    weights[0] = jnp.where(line == 0, v[...], c_near)
-    row = lax.broadcasted_iota(jnp.int32, (128, rows), 0)
-    scale[...] = jnp.where(row == 0, v[...], jnp.where(row == 1, c_near, c_far)).T
-
-
-def gram(pos, prod, weights, q, bands, send, out, sent, prod_here, weights_here, sems):
-    del bands, send, sent
+    weights[0] = jnp.where(line == 0, v[...], jnp.where(line == 1, c_near, c_far))
+
+
+def gram(pos, prod, weights, q, bands, out, here, sem):
+    del bands
     parts, kinds, rows, rank = out.shape
-    copies = [pltpu.make_async_copy(weights, weights_here, sems.at[STEPS])]
-    copies += [pltpu.make_async_copy(prod.at[k], prod_here.at[k], sems.at[k]) for k in range(STEPS)]
-    for copy in copies:
-        copy.start()
-    copies[0].wait()
     left = []
     for k in range(STEPS):
-        copies[k + 1].wait()
-        block = prod_here[k].astype(F32)
-        left.append(jnp.concatenate([(block * weights_here[k, n : n + 1]).astype(BF) for n in range(kinds)], axis=0))
+        block = prod[k].astype(F32)
+        left.append(jnp.concatenate([(block * weights[k, n : n + 1]).astype(BF) for n in range(kinds)], axis=0))
     total = jnp.dot(jnp.concatenate(left, axis=1), q[1 - pos[0]], preferred_element_type=F32)
     total = total.astype(BF)
     for kind in range(kinds):
         for part in range(parts):
             at = kind * rank + part * rows
-            out[part, kind] = total[at : at + rows]
+            here[part, kind] = total[at : at + rows]
+    copy = pltpu.make_async_copy(here, out, sem)
+    copy.start()
+    copy.wait()
 
 
 def total_of(x):
@@ -101,19 +97,26 @@
         out[k] = res
 
 
-def finish(pos, mats, q_near, q_far, scale, out, here, sems):
+def finish(pos, mats, q_near, q_far, weights, out, here, sems):
     near = pos[0]
     slots, parts, kinds, rows, rank = mats.shape
     width = here.shape[2]
 
     def pick(slot, kind):
-        return mats[slot, :, kind].reshape(parts * rows, rank)
+        return mats[1 - slot, :, kind].reshape(parts * rows, rank)
 
     def across(q, m):
         return lax.dot_general(q, m, (((1,), (1,)), ((), ())), preferred_element_type=F32)
 
     def straight(q, m):
         return jnp.dot(q, m, preferred_element_type=F32)
+
+    def column(k, n):
+        return jnp.concatenate([jnp.broadcast_to(weights[k, n : n + 1], (128, width)).T] * (rank // 128), axis=1)
+
+    def far_block(k):
+        block = q_far[k * width : min((k + 1) * width, q_far.shape[0])]
+        return block
 
     copies = []
     for which, slot, multiply in ((0, near, across), (1, 1 - near, straight)):
@@ -121,8 +124,8 @@
         by_v = pick(slot, 1)
         for k in range(STEPS):
             span = pl.ds(k * width, width)
-            q = q_near[1 - near, span] if which == 0 else q_far[span]
-            res = scale[span, 1 + which : 2 + which] * multiply(q, by_c) + scale[span, 0:1] * multiply(q, by_v)
+            q = q_near[1 - near, span] if which == 0 else far_block(k)
+            res = column(k, 1 + which) * multiply(q, by_c) + column(k, 0) * multiply(q, by_v)
             here[which, k] = res.astype(BF)
             copy = pltpu.make_async_copy(here.at[which, k], out.at[slot, span], sems.at[which, k])
             copy.start()
@@ -142,7 +145,7 @@
     v = probe_vector.reshape(1, rows)
 
     met = exchange(factors, "xh")
-    prod, weights, send, scale, bands = pl.pallas_call(
+    prod, weights, send, bands = pl.pallas_call(
         prepare,
         grid_spec=pltpu.PrefetchScalarGridSpec(
             num_scalar_prefetch=1,
@@ -157,7 +160,6 @@
                 pl.BlockSpec((1, rank, quarter), lambda i, s: (i, 0, 0)),
                 pl.BlockSpec((1, 8, quarter), lambda i, s: (i, 0, 0)),
                 pl.BlockSpec((quarter, rank), lambda i, s: (i, 0)),
-                pl.BlockSpec((quarter, 128), lambda i, s: (i, 0)),
                 pl.BlockSpec((16, rank), lambda i, s: (0, 0)),
             ],
         ),
@@ -165,7 +167,6 @@
             jax.ShapeDtypeStruct((STEPS, rank, quarter), BF),
             jax.ShapeDtypeStruct((STEPS, 8, quarter), F32),
             jax.ShapeDtypeStruct((rows, rank), BF),
-            jax.ShapeDtypeStruct((rows, 128), F32),
             jax.ShapeDtypeStruct((16, rank), BF),
         ],
         compiler_params=PARAMS,
@@ -173,21 +174,16 @@
     )(pos, factors, tridiag, v, cotangent)
     bands = lax.ppermute(bands, "xh", SWAP)
 
-    part, send = pl.pallas_call(
+    part = pl.pallas_call(
         gram,
-        in_specs=[SMEM, HBM, HBM, VMEM, ANY, ANY],
-        out_specs=[VMEM, ANY],
-        out_shape=[jax.ShapeDtypeStruct((reducers, 2, piece, rank), BF), like(send)],
-        scratch_shapes=[
-            pltpu.VMEM(prod.shape, BF),
-            pltpu.VMEM(weights.shape, F32),
-            pltpu.SemaphoreType.DMA((STEPS + 1,)),
-        ],
-        input_output_aliases={5: 1},
+        in_specs=[SMEM, VMEM, VMEM, VMEM, ANY],
+        out_specs=ANY,
+        out_shape=jax.ShapeDtypeStruct((reducers, 2, piece, rank), BF),
+        scratch_shapes=[pltpu.VMEM((reducers, 2, piece, rank), BF), pltpu.SemaphoreType.DMA(())],
         compiler_params=PARAMS,
         name="gram",
-    )(pos, prod, weights, met, bands, send)
-    got = exchange(part, REDUCE)
+    )(pos, prod, weights, met, bands)
+    got = exchange(part, REDUCE, list(range(reducers))[::-1])
     far = lax.ppermute(send, "xh", SWAP)
 
     some = pl.pallas_call(
@@ -198,7 +194,7 @@
         compiler_params=PARAMS,
         name="add_up",
     )(got)
-    got = exchange(some, RING)
+    got = exchange(some, RING, [(k + ring // 2) % ring for k in range(ring)])
 
     total = pl.pallas_call(
         add_up_through,
@@ -208,7 +204,7 @@
         compiler_params=PARAMS,
         name="add_up_through",
     )(got, bands, far)
-    mats = exchange(total, SPREAD).reshape(2, reducers, 2, piece, rank)
+    mats = exchange(total, SPREAD, list(range(spread))[::-1]).reshape(2, reducers, 2, piece, rank)
 
     return pl.pallas_call(
         finish,
@@ -218,7 +214,7 @@
         scratch_shapes=[pltpu.VMEM((2, STEPS, quarter, rank), BF), pltpu.SemaphoreType.DMA((2, STEPS))],
         compiler_params=PARAMS,
         name="finish",
-    )(pos, mats, met, far, scale)
+    )(pos, mats, met, far, weights)
 
 
 def solution(mesh):

time: 96.1 us -> 86.4 us (0.90)
  waiting for transfers between devices: 31.8 us -> 22.6 us
  local copies, waits for them, and re-layouts: 6.45 us -> 2.56 us
  starting transfers between devices: 33.8 us -> 37.6 us
    all_to_all x3, waiting for transfers between devices: 8.45 us -> 0.01 us  [exchange(): return lax.all_to_all(x, axes, 0, 0, tiled=True, axis_index_groups=groups)]
    unnamed x20 -> x10, local copies, waits for them, and re-layouts: 6.45 us -> 2.56 us
    all_to_all x3, starting transfers between devices: 26.8 us -> 30.5 us  [exchange(): return lax.all_to_all(x, axes, 0, 0, tiled=True, axis_index_groups=groups)]
    ppermute x1, waiting for transfers between devices: 7.24 us -> 5.52 us  [per_device(): far = lax.ppermute(send, 'xh', SWAP)]
    ppermute x1, waiting for transfers between devices: 16.1 us -> 17.1 us  [per_device(): bands = lax.ppermute(bands, 'xh', SWAP)]
  transfers between devices with their start and end apart: 5 -> 5, of which waited for: 4 -> 2; matrix products, arithmetic and copies ran while one was open for 0% -> 0% of each run, Pallas kernels for 3% -> 3%
where the time goes in v3:
time: 86.4 us; the launch traced here: 85.9 us
  starting transfers between devices  37.6 us (44%)
  waiting for transfers between devices  22.6 us (26%)
  blocking collectives  15.6 us (18%)
  Pallas kernels  7.3 us (8%)
  local copies, waits for them, and re-layouts  2.56 us (3%)
    all_to_all x3, starting transfers between devices, exchange(): return lax.all_to_all(x, axes, 0, 0, tiled=True, axis_index_groups=groups)  30.5 us
    ppermute x1, waiting for transfers between devices, per_device(): bands = lax.ppermute(bands, 'xh', SWAP)  17.1 us
    all_to_all x1, blocking collectives, exchange(): return lax.all_to_all(x, axes, 0, 0, tiled=True, axis_index_groups=groups)  15.6 us
    ppermute x1, waiting for transfers between devices, per_device(): far = lax.ppermute(send, 'xh', SWAP)  5.52 us
    ppermute x1, starting transfers between devices, per_device(): far = lax.ppermute(send, 'xh', SWAP)  5.13 us
    pallas_call x1, Pallas kernels, per_device(): pl.pallas_call(finish, in_specs=[SMEM, VMEM, VMEM, VMEM, VMEM], out_specs...  2.62 us
    unnamed x10, local copies, waits for them, and re-layouts  2.56 us
    pallas_call x1, Pallas kernels, per_device(): pl.pallas_call(gram, in_specs=[SMEM, VMEM, VMEM, VMEM, ANY], out_specs=AN...  1.98 us
  transfers between devices with their start and end apart: 5, of which 2 were waited for; matrix products, arithmetic and copies ran while one was open for 0% of the time, Pallas kernels for 3%

profile of v3, /device:TPU:6, one launch (start us, length us, event | category | flops | bytes accessed | tf_op | source)
XLA Modules:
  0.0 85.9 jit_solution(527816353722294763)
XLA Ops:
  0.0 0.0 copy-start.2
  0.0 5.3 %all-to-all-start = ((bf16[2,2048,256]{2,1,0:T(8,128)(2,1)}), bf16[2,2048,256]{2,1,0:T(8,128)(2,1)S(1)}, u32[]{:S(2)}, u32[]{:S(2)}) async-start(bf16[2,2048,256]{2,1,0:T(8,128)(2,1)} %q.1), calls=%async_computation | async-start | bytes 4194304 | tf_op jit(solution)/shard_map/all_to_all | solution.py:28
  5.3 0.1 pad_add_fusion.pos
  5.4 0.0 copy-done.2
  5.4 0.0 copy-done.3
  5.4 0.0 copy-done.1
  5.4 1.6 %copy-done = bf16[2,2048,256]{2,1,0:T(8,128)(2,1)S(1)} copy-done((bf16[2,2048,256]{2,1,0:T(8,128)(2,1)S(1)}, bf16[2,2048,256]{2,1,0:T(8,128)(2,1)}, u32[]{:S(2)}) %copy-start) | copy-done | bytes 2097176
  7.0 1.9 %prepare.1 = (bf16[4,256,512]{2,1,0:T(8,128)(2,1)S(1)}, f32[4,8,512]{2,1,0:T(8,128)S(1)}, bf16[2048,256]{1,0:T(8,128)(2,1)S(1)}, bf16[16,256]{1,0:T(8,128)(2,1)S(1)}) custom-call(s32[2]{0:T(128)S(1)} %pad_add_fusion.pos, bf16[2,2048,256]{2,1,0:T(8,128)(2,1)S(1)} %copy-done, bf16[2,256,256]{2,1,0:T(8,128)(2,1)S(1)} %copy-done.1, f32[1,2048]{1,0:T(1,128)S(1)} %bitcast.5, ...), custom_call_target="tpu_custom_call" | custom-call | tf_op jit(solution)/shard_map/prepare/pallas_call | solution.py:148
  8.9 0.0 copy-start.4
  8.9 1.0 %copy-done.4 = bf16[2048,256]{1,0:T(8,128)(2,1)} copy-done((bf16[2048,256]{1,0:T(8,128)(2,1)}, bf16[2048,256]{1,0:T(8,128)(2,1)S(1)}, u32[]{:S(2)}) %copy-start.4) | copy-done | bytes 1048600
  9.8 1.9 %collective-permute-start = (bf16[16,256]{1,0:T(8,128)(2,1)S(1)}, bf16[16,256]{1,0:T(8,128)(2,1)S(1)}, u32[]{:S(2)}, u32[]{:S(2)}) collective-permute-start(bf16[16,256]{1,0:T(8,128)(2,1)S(1)} %get-tuple-element.11), channel_id=1, source_target_pairs={{0,2},{2,0},{1,3},{3,1},{4,6},{6,4},{5,7},{7,5},{8,10},{10,8},{9,1... | collective-permute-start | bytes 24584 | tf_op jit(solution)/shard_map/ppermute | solution.py:175
  11.7 17.1 %collective-permute-done.bands = bf16[16,256]{1,0:T(8,128)(2,1)S(1)} collective-permute-done((bf16[16,256]{1,0:T(8,128)(2,1)S(1)}, bf16[16,256]{1,0:T(8,128)(2,1)S(1)}, u32[]{:S(2)}, u32[]{:S(2)}) %collective-permute-start) | collective-permute-done | bytes 8224 | tf_op jit(solution)/shard_map/ppermute | solution.py:175
  28.9 0.0 all-to-all-done.q.q_near
  28.9 2.0 %gram.1 = bf16[16,2,16,256]{3,2,1,0:T(8,128)(2,1)} custom-call(s32[2]{0:T(128)S(1)} %pad_add_fusion.pos, bf16[4,256,512]{2,1,0:T(8,128)(2,1)S(1)} %get-tuple-element.9.prod, f32[4,8,512]{2,1,0:T(8,128)S(1)} %get-tuple-element.10.weights, bf16[2,2048,256]{2,1,0:T(8,128)(2,1)S(1)} %all-to-all-done.q.q_near, bf16[16,256]{1,0:T(8,128)(2,1)S(1)} %collective-permute-done.bands), custom_call_target="tpu_custom_call" | custom-call | tf_op jit(solution)/shard_map/gram/pallas_call | solution.py:177
  30.9 7.8 %all-to-all-start.1 = ((bf16[16,2,16,256]{3,2,1,0:T(8,128)(2,1)}), bf16[16,2,16,256]{3,2,1,0:T(8,128)(2,1)S(1)}, u32[]{:S(2)}, u32[]{:S(2)}) async-start(bf16[16,2,16,256]{3,2,1,0:T(8,128)(2,1)} %gram.1), calls=%async_computation.1 | async-start | bytes 524288 | tf_op jit(solution)/shard_map/all_to_all | solution.py:28
  38.6 5.1 %collective-permute-start.1 = (bf16[2048,256]{1,0:T(8,128)(2,1)}, bf16[2048,256]{1,0:T(8,128)(2,1)S(1)}, u32[]{:S(2)}, u32[]{:S(2)}) collective-permute-start(bf16[2048,256]{1,0:T(8,128)(2,1)} %copy-done.4), channel_id=1, source_target_pairs={{0,2},{2,0},{1,3},{3,1},{4,6},{6,4},{5,7},{7,5},{8,10},{10,8},{9,1... | collective-permute-start | bytes 3145736 | tf_op jit(solution)/shard_map/ppermute | solution.py:187
  43.8 0.0 all-to-all-done.1.x
  43.8 0.7 add_up.1
  44.5 17.5 %all-to-all-start.2 = ((bf16[8,2,16,256]{3,2,1,0:T(8,128)(2,1)}), bf16[8,2,16,256]{3,2,1,0:T(8,128)(2,1)S(1)}, u32[]{:S(2)}, u32[]{:S(2)}) async-start(bf16[8,2,16,256]{3,2,1,0:T(8,128)(2,1)} %add_up.1), calls=%async_computation.2 | async-start | bytes 262144 | tf_op jit(solution)/shard_map/all_to_all | solution.py:28
  62.0 5.5 %collective-permute-done.1.far.q_far = bf16[2048,256]{1,0:T(8,128)(2,1)S(1)} collective-permute-done((bf16[2048,256]{1,0:T(8,128)(2,1)}, bf16[2048,256]{1,0:T(8,128)(2,1)S(1)}, u32[]{:S(2)}, u32[]{:S(2)}) %collective-permute-start.1) | collective-permute-done | bytes 1048608 | tf_op jit(solution)/shard_map/ppermute | solution.py:187
  67.5 0.0 all-to-all-done.2.x
  67.5 0.1 add_up_through.1
  67.6 15.6 %all_to_all.20 = bf16[32,2,16,256]{3,2,1,0:T(8,128)(2,1)S(1)} all-to-all(bf16[32,2,16,256]{3,2,1,0:T(8,128)(2,1)S(1)} %add_up_through.1), channel_id=1, replica_groups={{286,282,278,274,30,26,22,18,270,266,262,258,14,10,6,2,284,280,276,272,..., dimensions={0} | all-to-all | bytes 1048576 | tf_op jit(solution)/shard_map/all_to_all | solution.py:28
  83.3 2.6 %finish.1 = bf16[2,2048,256]{2,1,0:T(8,128)(2,1)} custom-call(s32[2]{0:T(128)S(1)} %pad_add_fusion.pos, bf16[2,16,2,16,256]{4,3,2,1,0:T(8,128)(2,1)S(1)} %bitcast.4, bf16[2,2048,256]{2,1,0:T(8,128)(2,1)S(1)} %all-to-all-done.q.q_near, bf16[2048,256]{1,0:T(8,128)(2,1)S(1)} %collective-permute-done.1.far.q_far, f32[4,8,512]{2,1,0:T(8,128)S(1)} %get-tuple-element.10.weights), custom_call_target="tpu_custom_call" | custom-call | tf_op jit(solution)/shard_map/finish/pallas_call | solution.py:209
  (3 shorter events, 0.0 us)
Async XLA Ops:
  0.0 5.4 %copy-start.2 = (f32[4,2048]{1,0:T(4,128)S(1)}, f32[4,2048]{1,0:T(4,128)}, u32[]{:S(2)}) copy-start(f32[4,2048]{1,0:T(4,128)} %c.1) | copy-start | bytes 98308
  0.0 5.4 %copy-start.3 = (f32[2048]{0:T(1024)S(1)}, f32[2048]{0:T(1024)}, u32[]{:S(2)}) copy-start(f32[2048]{0:T(1024)} %param.6) | copy-start | bytes 24580
  0.0 5.4 %copy-start.1 = (bf16[2,256,256]{2,1,0:T(8,128)(2,1)S(1)}, bf16[2,256,256]{2,1,0:T(8,128)(2,1)}, u32[]{:S(2)}) copy-start(bf16[2,256,256]{2,1,0:T(8,128)(2,1)} %t.1) | copy-start | bytes 786436
  0.0 28.9 %all-to-all-start = ((bf16[2,2048,256]{2,1,0:T(8,128)(2,1)}), bf16[2,2048,256]{2,1,0:T(8,128)(2,1)S(1)}, u32[]{:S(2)}, u32[]{:S(2)}) async-start(bf16[2,2048,256]{2,1,0:T(8,128)(2,1)} %q.1), calls=%async_computation | async-start | bytes 4194304 | tf_op jit(solution)/shard_map/all_to_all | solution.py:28
  5.4 1.6 %copy-start = (bf16[2,2048,256]{2,1,0:T(8,128)(2,1)S(1)}, bf16[2,2048,256]{2,1,0:T(8,128)(2,1)}, u32[]{:S(2)}) copy-start(bf16[2,2048,256]{2,1,0:T(8,128)(2,1)} %q.1) | copy-start | bytes 6291460
  8.9 1.0 %copy-start.4 = (bf16[2048,256]{1,0:T(8,128)(2,1)}, bf16[2048,256]{1,0:T(8,128)(2,1)S(1)}, u32[]{:S(2)}) copy-start(bf16[2048,256]{1,0:T(8,128)(2,1)S(1)} %get-tuple-element.12) | copy-start | bytes 3145732
  9.8 19.0 %collective-permute-start = (bf16[16,256]{1,0:T(8,128)(2,1)S(1)}, bf16[16,256]{1,0:T(8,128)(2,1)S(1)}, u32[]{:S(2)}, u32[]{:S(2)}) collective-permute-start(bf16[16,256]{1,0:T(8,128)(2,1)S(1)} %get-tuple-element.11), channel_id=1, source_target_pairs={{0,2},{2,0},{1,3},{3,1},{4,6},{6,4},{5,7},{7,5},{8,10},{10,8},{9,1... | collective-permute-start | bytes 24584 | tf_op jit(solution)/shard_map/ppermute | solution.py:175
  30.9 12.9 %all-to-all-start.1 = ((bf16[16,2,16,256]{3,2,1,0:T(8,128)(2,1)}), bf16[16,2,16,256]{3,2,1,0:T(8,128)(2,1)S(1)}, u32[]{:S(2)}, u32[]{:S(2)}) async-start(bf16[16,2,16,256]{3,2,1,0:T(8,128)(2,1)} %gram.1), calls=%async_computation.1 | async-start | bytes 524288 | tf_op jit(solution)/shard_map/all_to_all | solution.py:28
  38.6 28.9 %collective-permute-start.1 = (bf16[2048,256]{1,0:T(8,128)(2,1)}, bf16[2048,256]{1,0:T(8,128)(2,1)S(1)}, u32[]{:S(2)}, u32[]{:S(2)}) collective-permute-start(bf16[2048,256]{1,0:T(8,128)(2,1)} %copy-done.4), channel_id=1, source_target_pairs={{0,2},{2,0},{1,3},{3,1},{4,6},{6,4},{5,7},{7,5},{8,10},{10,8},{9,1... | collective-permute-start | bytes 3145736 | tf_op jit(solution)/shard_map/ppermute | solution.py:187
  44.5 23.0 %all-to-all-start.2 = ((bf16[8,2,16,256]{3,2,1,0:T(8,128)(2,1)}), bf16[8,2,16,256]{3,2,1,0:T(8,128)(2,1)S(1)}, u32[]{:S(2)}, u32[]{:S(2)}) async-start(bf16[8,2,16,256]{3,2,1,0:T(8,128)(2,1)} %add_up.1), calls=%async_computation.2 | async-start | bytes 262144 | tf_op jit(solution)/shard_map/all_to_all | solution.py:28

commit v4 on v3

--- a/solution.py
+++ b/solution.py
@@ -72,6 +72,10 @@
     copy.wait()
 
 
+def hold(x, after, same):
+    del x, after, same
+
+
 def total_of(x):
     total = x[0].astype(F32)
     for k in range(1, x.shape[0]):
@@ -85,8 +89,7 @@
         out[k] = total
 
 
-def add_up_through(x, bands, far, out):
-    del far
+def add_up_through(x, bands, out):
     total = total_of(x)
     kinds, rows, rank = total.shape
     flat = total.reshape(kinds * rows, rank)
@@ -198,12 +201,21 @@
 
     total = pl.pallas_call(
         add_up_through,
-        in_specs=[VMEM, VMEM, ANY],
+        in_specs=[VMEM, VMEM],
         out_specs=VMEM,
         out_shape=jax.ShapeDtypeStruct((spread, 2, piece, rank), BF),
         compiler_params=PARAMS,
         name="add_up_through",
-    )(got, bands, far)
+    )(got, bands)
+    total = pl.pallas_call(
+        hold,
+        in_specs=[ANY, ANY],
+        out_specs=ANY,
+        out_shape=like(total),
+        input_output_aliases={0: 0},
+        compiler_params=PARAMS,
+        name="hold",
+    )(total, far)
     mats = exchange(total, SPREAD, list(range(spread))[::-1]).reshape(2, reducers, 2, piece, rank)
 
     return pl.pallas_call(

time: 86.4 us -> 86 us (level)
  blocking collectives: 15.6 us -> 37 us
  starting transfers between devices: 37.6 us -> 20.1 us
  waiting for transfers between devices: 22.6 us -> 18.7 us
    all_to_all x1 -> x2, blocking collectives: 15.6 us -> 37 us  [exchange(): return lax.all_to_all(x, axes, 0, 0, tiled=True, axis_index_groups=groups)]
    all_to_all x3 -> x2, starting transfers between devices: 30.5 us -> 13.1 us  [exchange(): return lax.all_to_all(x, axes, 0, 0, tiled=True, axis_index_groups=groups)]
    ppermute x1, waiting for transfers between devices: 5.52 us -> 1.55 us  [per_device(): far = lax.ppermute(send, 'xh', SWAP)]
  transfers between devices with their start and end apart: 5 -> 4, of which waited for: 2 -> 2; matrix products, arithmetic and copies ran while one was open for 0% -> 0% of each run, Pallas kernels for 3% -> 2%
where the time goes in v4:
time: 86 us; the launch traced here: 85.2 us
  blocking collectives  37 us (43%)
  starting transfers between devices  20.1 us (23%)
  waiting for transfers between devices  18.7 us (22%)
  Pallas kernels  6.66 us (8%)
  local copies, waits for them, and re-layouts  2.56 us (3%)
    all_to_all x2, blocking collectives, exchange(): return lax.all_to_all(x, axes, 0, 0, tiled=True, axis_index_groups=groups)  37 us
    ppermute x1, waiting for transfers between devices, per_device(): bands = lax.ppermute(bands, 'xh', SWAP)  17.1 us
    all_to_all x2, starting transfers between devices, exchange(): return lax.all_to_all(x, axes, 0, 0, tiled=True, axis_index_groups=groups)  13.1 us
    ppermute x1, starting transfers between devices, per_device(): far = lax.ppermute(send, 'xh', SWAP)  5.13 us
    pallas_call x1, Pallas kernels, per_device(): pl.pallas_call(finish, in_specs=[SMEM, VMEM, VMEM, VMEM, VMEM], out_specs...  2.62 us
    unnamed x10, local copies, waits for them, and re-layouts  2.56 us
    pallas_call x1, Pallas kernels, per_device(): pl.pallas_call(gram, in_specs=[SMEM, VMEM, VMEM, VMEM, ANY], out_specs=AN...  1.99 us
    ppermute x1, starting transfers between devices, per_device(): bands = lax.ppermute(bands, 'xh', SWAP)  1.92 us
  transfers between devices with their start and end apart: 4, of which 2 were waited for; matrix products, arithmetic and copies ran while one was open for 0% of the time, Pallas kernels for 2%

profile of v4, /device:TPU:6, one launch (start us, length us, event | category | flops | bytes accessed | tf_op | source)
XLA Modules:
  0.0 85.2 jit_solution(15949156950130169984)
XLA Ops:
  0.0 0.0 copy-start.2
  0.0 0.0 copy-start.3
  0.0 0.0 copy-start.1
  0.0 5.3 %all-to-all-start = ((bf16[2,2048,256]{2,1,0:T(8,128)(2,1)}), bf16[2,2048,256]{2,1,0:T(8,128)(2,1)S(1)}, u32[]{:S(2)}, u32[]{:S(2)}) async-start(bf16[2,2048,256]{2,1,0:T(8,128)(2,1)} %q.1), calls=%async_computation | async-start | bytes 4194304 | tf_op jit(solution)/shard_map/all_to_all | solution.py:28
  5.3 0.1 pad_add_fusion.pos
  5.4 0.0 copy-done.2
  5.4 0.0 copy-done.3
  5.4 0.0 copy-done.1
  5.4 1.6 %copy-done = bf16[2,2048,256]{2,1,0:T(8,128)(2,1)S(1)} copy-done((bf16[2,2048,256]{2,1,0:T(8,128)(2,1)S(1)}, bf16[2,2048,256]{2,1,0:T(8,128)(2,1)}, u32[]{:S(2)}) %copy-start) | copy-done | bytes 2097176
  7.0 1.9 %prepare.1 = (bf16[4,256,512]{2,1,0:T(8,128)(2,1)S(1)}, f32[4,8,512]{2,1,0:T(8,128)S(1)}, bf16[2048,256]{1,0:T(8,128)(2,1)S(1)}, bf16[16,256]{1,0:T(8,128)(2,1)S(1)}) custom-call(s32[2]{0:T(128)S(1)} %pad_add_fusion.pos, bf16[2,2048,256]{2,1,0:T(8,128)(2,1)S(1)} %copy-done, bf16[2,256,256]{2,1,0:T(8,128)(2,1)S(1)} %copy-done.1, f32[1,2048]{1,0:T(1,128)S(1)} %bitcast.5, ...), custom_call_target="tpu_custom_call" | custom-call | tf_op jit(solution)/shard_map/prepare/pallas_call | solution.py:151
  8.9 0.0 copy-start.4
  8.9 1.0 %copy-done.4 = bf16[2048,256]{1,0:T(8,128)(2,1)} copy-done((bf16[2048,256]{1,0:T(8,128)(2,1)}, bf16[2048,256]{1,0:T(8,128)(2,1)S(1)}, u32[]{:S(2)}) %copy-start.4) | copy-done | bytes 1048600
  9.8 1.9 %collective-permute-start = (bf16[16,256]{1,0:T(8,128)(2,1)S(1)}, bf16[16,256]{1,0:T(8,128)(2,1)S(1)}, u32[]{:S(2)}, u32[]{:S(2)}) collective-permute-start(bf16[16,256]{1,0:T(8,128)(2,1)S(1)} %get-tuple-element.11), channel_id=1, source_target_pairs={{0,2},{2,0},{1,3},{3,1},{4,6},{6,4},{5,7},{7,5},{8,10},{10,8},{9,1... | collective-permute-start | bytes 24584 | tf_op jit(solution)/shard_map/ppermute | solution.py:178
  11.7 17.1 %collective-permute-done.bands = bf16[16,256]{1,0:T(8,128)(2,1)S(1)} collective-permute-done((bf16[16,256]{1,0:T(8,128)(2,1)S(1)}, bf16[16,256]{1,0:T(8,128)(2,1)S(1)}, u32[]{:S(2)}, u32[]{:S(2)}) %collective-permute-start) | collective-permute-done | bytes 8224 | tf_op jit(solution)/shard_map/ppermute | solution.py:178
  28.9 0.0 all-to-all-done.q.q_near
  28.9 2.0 %gram.1 = bf16[16,2,16,256]{3,2,1,0:T(8,128)(2,1)} custom-call(s32[2]{0:T(128)S(1)} %pad_add_fusion.pos, bf16[4,256,512]{2,1,0:T(8,128)(2,1)S(1)} %get-tuple-element.9.prod, f32[4,8,512]{2,1,0:T(8,128)S(1)} %get-tuple-element.10.weights, bf16[2,2048,256]{2,1,0:T(8,128)(2,1)S(1)} %all-to-all-done.q.q_near, bf16[16,256]{1,0:T(8,128)(2,1)S(1)} %collective-permute-done.bands), custom_call_target="tpu_custom_call" | custom-call | tf_op jit(solution)/shard_map/gram/pallas_call | solution.py:180
  30.9 7.8 %all-to-all-start.1 = ((bf16[16,2,16,256]{3,2,1,0:T(8,128)(2,1)}), bf16[16,2,16,256]{3,2,1,0:T(8,128)(2,1)S(1)}, u32[]{:S(2)}, u32[]{:S(2)}) async-start(bf16[16,2,16,256]{3,2,1,0:T(8,128)(2,1)} %gram.1), calls=%async_computation.1 | async-start | bytes 524288 | tf_op jit(solution)/shard_map/all_to_all | solution.py:28
  38.6 5.1 %collective-permute-start.1 = (bf16[2048,256]{1,0:T(8,128)(2,1)}, bf16[2048,256]{1,0:T(8,128)(2,1)S(1)}, u32[]{:S(2)}, u32[]{:S(2)}) collective-permute-start(bf16[2048,256]{1,0:T(8,128)(2,1)} %copy-done.4), channel_id=1, source_target_pairs={{0,2},{2,0},{1,3},{3,1},{4,6},{6,4},{5,7},{7,5},{8,10},{10,8},{9,1... | collective-permute-start | bytes 3145736 | tf_op jit(solution)/shard_map/ppermute | solution.py:190
  43.8 0.0 all-to-all-done.1.x
  43.8 22.0 %all_to_all.20.x = bf16[8,2,16,256]{3,2,1,0:T(8,128)(2,1)S(1)} all-to-all(bf16[8,2,16,256]{3,2,1,0:T(8,128)(2,1)S(1)} %add_up.1), channel_id=1, replica_groups={{128,160,192,224,0,32,64,96},{129,161,193,225,1,33,65,97},{130,162,194,..., dimensions={0} | all-to-all | bytes 262144 | tf_op jit(solution)/shard_map/all_to_all | solution.py:28
  65.8 0.1 add_up_through.1.x
  65.9 1.5 %collective-permute-done.1.after.q_far = bf16[2048,256]{1,0:T(8,128)(2,1)S(1)} collective-permute-done((bf16[2048,256]{1,0:T(8,128)(2,1)}, bf16[2048,256]{1,0:T(8,128)(2,1)S(1)}, u32[]{:S(2)}, u32[]{:S(2)}) %collective-permute-start.1) | collective-permute-done | bytes 1048608 | tf_op jit(solution)/shard_map/ppermute | solution.py:190
  67.5 15.1 %all_to_all.21 = bf16[32,2,16,256]{3,2,1,0:T(8,128)(2,1)S(1)} all-to-all(bf16[32,2,16,256]{3,2,1,0:T(8,128)(2,1)S(1)} %hold.1), channel_id=1, replica_groups={{286,282,278,274,30,26,22,18,270,266,262,258,14,10,6,2,284,280,276,272,..., dimensions={0} | all-to-all | bytes 1048576 | tf_op jit(solution)/shard_map/all_to_all | solution.py:28
  82.6 2.6 %finish.1 = bf16[2,2048,256]{2,1,0:T(8,128)(2,1)} custom-call(s32[2]{0:T(128)S(1)} %pad_add_fusion.pos, bf16[2,16,2,16,256]{4,3,2,1,0:T(8,128)(2,1)S(1)} %bitcast.4, bf16[2,2048,256]{2,1,0:T(8,128)(2,1)S(1)} %all-to-all-done.q.q_near, bf16[2048,256]{1,0:T(8,128)(2,1)S(1)} %collective-permute-done.1.after.q_far, f32[4,8,512]{2,1,0:T(8,128)S(1)} %get-tuple-element.10.weights), custom_call_target="tpu_custom_call" | custom-call | tf_op jit(solution)/shard_map/finish/pallas_call | solution.py:221
  (3 shorter events, 0.0 us)
Async XLA Ops:
  0.0 5.4 %copy-start.2 = (f32[4,2048]{1,0:T(4,128)S(1)}, f32[4,2048]{1,0:T(4,128)}, u32[]{:S(2)}) copy-start(f32[4,2048]{1,0:T(4,128)} %c.1) | copy-start | bytes 98308
  0.0 5.4 %copy-start.3 = (f32[2048]{0:T(1024)S(1)}, f32[2048]{0:T(1024)}, u32[]{:S(2)}) copy-start(f32[2048]{0:T(1024)} %param.6) | copy-start | bytes 24580
  0.0 5.4 %copy-start.1 = (bf16[2,256,256]{2,1,0:T(8,128)(2,1)S(1)}, bf16[2,256,256]{2,1,0:T(8,128)(2,1)}, u32[]{:S(2)}) copy-start(bf16[2,256,256]{2,1,0:T(8,128)(2,1)} %t.1) | copy-start | bytes 786436
  0.0 28.9 %all-to-all-start = ((bf16[2,2048,256]{2,1,0:T(8,128)(2,1)}), bf16[2,2048,256]{2,1,0:T(8,128)(2,1)S(1)}, u32[]{:S(2)}, u32[]{:S(2)}) async-start(bf16[2,2048,256]{2,1,0:T(8,128)(2,1)} %q.1), calls=%async_computation | async-start | bytes 4194304 | tf_op jit(solution)/shard_map/all_to_all | solution.py:28
  5.4 1.6 %copy-start = (bf16[2,2048,256]{2,1,0:T(8,128)(2,1)S(1)}, bf16[2,2048,256]{2,1,0:T(8,128)(2,1)}, u32[]{:S(2)}) copy-start(bf16[2,2048,256]{2,1,0:T(8,128)(2,1)} %q.1) | copy-start | bytes 6291460
  8.9 1.0 %copy-start.4 = (bf16[2048,256]{1,0:T(8,128)(2,1)}, bf16[2048,256]{1,0:T(8,128)(2,1)S(1)}, u32[]{:S(2)}) copy-start(bf16[2048,256]{1,0:T(8,128)(2,1)S(1)} %get-tuple-element.12) | copy-start | bytes 3145732
  9.8 19.0 %collective-permute-start = (bf16[16,256]{1,0:T(8,128)(2,1)S(1)}, bf16[16,256]{1,0:T(8,128)(2,1)S(1)}, u32[]{:S(2)}, u32[]{:S(2)}) collective-permute-start(bf16[16,256]{1,0:T(8,128)(2,1)S(1)} %get-tuple-element.11), channel_id=1, source_target_pairs={{0,2},{2,0},{1,3},{3,1},{4,6},{6,4},{5,7},{7,5},{8,10},{10,8},{9,1... | collective-permute-start | bytes 24584 | tf_op jit(solution)/shard_map/ppermute | solution.py:178
  30.9 12.9 %all-to-all-start.1 = ((bf16[16,2,16,256]{3,2,1,0:T(8,128)(2,1)}), bf16[16,2,16,256]{3,2,1,0:T(8,128)(2,1)S(1)}, u32[]{:S(2)}, u32[]{:S(2)}) async-start(bf16[16,2,16,256]{3,2,1,0:T(8,128)(2,1)} %gram.1), calls=%async_computation.1 | async-start | bytes 524288 | tf_op jit(solution)/shard_map/all_to_all | solution.py:28
  38.6 28.9 %collective-permute-start.1 = (bf16[2048,256]{1,0:T(8,128)(2,1)}, bf16[2048,256]{1,0:T(8,128)(2,1)S(1)}, u32[]{:S(2)}, u32[]{:S(2)}) collective-permute-start(bf16[2048,256]{1,0:T(8,128)(2,1)} %copy-done.4), channel_id=1, source_target_pairs={{0,2},{2,0},{1,3},{3,1},{4,6},{6,4},{5,7},{7,5},{8,10},{10,8},{9,1... | collective-permute-start | bytes 3145736 | tf_op jit(solution)/shard_map/ppermute | solution.py:190

commit v5 on v4

--- a/solution.py
+++ b/solution.py
@@ -59,8 +59,7 @@
     parts, kinds, rows, rank = out.shape
     left = []
     for k in range(STEPS):
-        block = prod[k].astype(F32)
-        left.append(jnp.concatenate([(block * weights[k, n : n + 1]).astype(BF) for n in range(kinds)], axis=0))
+        left.append(jnp.concatenate([prod[k] * weights[k, n : n + 1].astype(BF) for n in range(kinds)], axis=0))
     total = jnp.dot(jnp.concatenate(left, axis=1), q[1 - pos[0]], preferred_element_type=F32)
     total = total.astype(BF)
     for kind in range(kinds):

time: 86 us -> 86 us (level)
  no operation moved by 1% of the time
where the time goes in v5:
time: 86 us; the launch traced here: 85.2 us
  blocking collectives  37 us (43%)
  starting transfers between devices  20.1 us (23%)
  waiting for transfers between devices  18.7 us (22%)
  Pallas kernels  6.64 us (8%)
  local copies, waits for them, and re-layouts  2.56 us (3%)
    all_to_all x2, blocking collectives, exchange(): return lax.all_to_all(x, axes, 0, 0, tiled=True, axis_index_groups=groups)  37 us
    ppermute x1, waiting for transfers between devices, per_device(): bands = lax.ppermute(bands, 'xh', SWAP)  17.1 us
    all_to_all x2, starting transfers between devices, exchange(): return lax.all_to_all(x, axes, 0, 0, tiled=True, axis_index_groups=groups)  13.1 us
    ppermute x1, starting transfers between devices, per_device(): far = lax.ppermute(send, 'xh', SWAP)  5.13 us
    pallas_call x1, Pallas kernels, per_device(): pl.pallas_call(finish, in_specs=[SMEM, VMEM, VMEM, VMEM, VMEM], out_specs...  2.62 us
    unnamed x10, local copies, waits for them, and re-layouts  2.56 us
    pallas_call x1, Pallas kernels, per_device(): pl.pallas_call(gram, in_specs=[SMEM, VMEM, VMEM, VMEM, ANY], out_specs=AN...  1.98 us
    ppermute x1, starting transfers between devices, per_device(): bands = lax.ppermute(bands, 'xh', SWAP)  1.92 us
  transfers between devices with their start and end apart: 4, of which 2 were waited for; matrix products, arithmetic and copies ran while one was open for 0% of the time, Pallas kernels for 2%

profile of v5, /device:TPU:6, one launch (start us, length us, event | category | flops | bytes accessed | tf_op | source)
XLA Modules:
  0.0 85.2 jit_solution(2045436507911860481)
XLA Ops:
  0.0 0.0 copy-start.2
  0.0 0.0 copy-start.3
  0.0 0.0 copy-start.1
  0.0 5.3 %all-to-all-start = ((bf16[2,2048,256]{2,1,0:T(8,128)(2,1)}), bf16[2,2048,256]{2,1,0:T(8,128)(2,1)S(1)}, u32[]{:S(2)}, u32[]{:S(2)}) async-start(bf16[2,2048,256]{2,1,0:T(8,128)(2,1)} %q.1), calls=%async_computation | async-start | bytes 4194304 | tf_op jit(solution)/shard_map/all_to_all | solution.py:28
  5.3 0.1 pad_add_fusion.pos
  5.4 0.0 copy-done.2
  5.4 0.0 copy-done.3
  5.4 0.0 copy-done.1
  5.4 1.6 %copy-done = bf16[2,2048,256]{2,1,0:T(8,128)(2,1)S(1)} copy-done((bf16[2,2048,256]{2,1,0:T(8,128)(2,1)S(1)}, bf16[2,2048,256]{2,1,0:T(8,128)(2,1)}, u32[]{:S(2)}) %copy-start) | copy-done | bytes 2097176
  7.0 1.9 %prepare.1 = (bf16[4,256,512]{2,1,0:T(8,128)(2,1)S(1)}, f32[4,8,512]{2,1,0:T(8,128)S(1)}, bf16[2048,256]{1,0:T(8,128)(2,1)S(1)}, bf16[16,256]{1,0:T(8,128)(2,1)S(1)}) custom-call(s32[2]{0:T(128)S(1)} %pad_add_fusion.pos, bf16[2,2048,256]{2,1,0:T(8,128)(2,1)S(1)} %copy-done, bf16[2,256,256]{2,1,0:T(8,128)(2,1)S(1)} %copy-done.1, f32[1,2048]{1,0:T(1,128)S(1)} %bitcast.5, ...), custom_call_target="tpu_custom_call" | custom-call | tf_op jit(solution)/shard_map/prepare/pallas_call | solution.py:150
  8.9 0.0 copy-start.4
  8.9 1.0 %copy-done.4 = bf16[2048,256]{1,0:T(8,128)(2,1)} copy-done((bf16[2048,256]{1,0:T(8,128)(2,1)}, bf16[2048,256]{1,0:T(8,128)(2,1)S(1)}, u32[]{:S(2)}) %copy-start.4) | copy-done | bytes 1048600
  9.8 1.9 %collective-permute-start = (bf16[16,256]{1,0:T(8,128)(2,1)S(1)}, bf16[16,256]{1,0:T(8,128)(2,1)S(1)}, u32[]{:S(2)}, u32[]{:S(2)}) collective-permute-start(bf16[16,256]{1,0:T(8,128)(2,1)S(1)} %get-tuple-element.11), channel_id=1, source_target_pairs={{0,2},{2,0},{1,3},{3,1},{4,6},{6,4},{5,7},{7,5},{8,10},{10,8},{9,1... | collective-permute-start | bytes 24584 | tf_op jit(solution)/shard_map/ppermute | solution.py:177
  11.7 17.1 %collective-permute-done.bands = bf16[16,256]{1,0:T(8,128)(2,1)S(1)} collective-permute-done((bf16[16,256]{1,0:T(8,128)(2,1)S(1)}, bf16[16,256]{1,0:T(8,128)(2,1)S(1)}, u32[]{:S(2)}, u32[]{:S(2)}) %collective-permute-start) | collective-permute-done | bytes 8224 | tf_op jit(solution)/shard_map/ppermute | solution.py:177
  28.9 0.0 all-to-all-done.q.q_near
  28.9 2.0 %gram.1 = bf16[16,2,16,256]{3,2,1,0:T(8,128)(2,1)} custom-call(s32[2]{0:T(128)S(1)} %pad_add_fusion.pos, bf16[4,256,512]{2,1,0:T(8,128)(2,1)S(1)} %get-tuple-element.9.prod, f32[4,8,512]{2,1,0:T(8,128)S(1)} %get-tuple-element.10.weights, bf16[2,2048,256]{2,1,0:T(8,128)(2,1)S(1)} %all-to-all-done.q.q_near, bf16[16,256]{1,0:T(8,128)(2,1)S(1)} %collective-permute-done.bands), custom_call_target="tpu_custom_call" | custom-call | tf_op jit(solution)/shard_map/gram/pallas_call | solution.py:179
  30.9 7.8 %all-to-all-start.1 = ((bf16[16,2,16,256]{3,2,1,0:T(8,128)(2,1)}), bf16[16,2,16,256]{3,2,1,0:T(8,128)(2,1)S(1)}, u32[]{:S(2)}, u32[]{:S(2)}) async-start(bf16[16,2,16,256]{3,2,1,0:T(8,128)(2,1)} %gram.1), calls=%async_computation.1 | async-start | bytes 524288 | tf_op jit(solution)/shard_map/all_to_all | solution.py:28
  38.6 5.1 %collective-permute-start.1 = (bf16[2048,256]{1,0:T(8,128)(2,1)}, bf16[2048,256]{1,0:T(8,128)(2,1)S(1)}, u32[]{:S(2)}, u32[]{:S(2)}) collective-permute-start(bf16[2048,256]{1,0:T(8,128)(2,1)} %copy-done.4), channel_id=1, source_target_pairs={{0,2},{2,0},{1,3},{3,1},{4,6},{6,4},{5,7},{7,5},{8,10},{10,8},{9,1... | collective-permute-start | bytes 3145736 | tf_op jit(solution)/shard_map/ppermute | solution.py:189
  43.8 0.0 all-to-all-done.1.x
  43.8 21.9 %all_to_all.20.x = bf16[8,2,16,256]{3,2,1,0:T(8,128)(2,1)S(1)} all-to-all(bf16[8,2,16,256]{3,2,1,0:T(8,128)(2,1)S(1)} %add_up.1), channel_id=1, replica_groups={{128,160,192,224,0,32,64,96},{129,161,193,225,1,33,65,97},{130,162,194,..., dimensions={0} | all-to-all | bytes 262144 | tf_op jit(solution)/shard_map/all_to_all | solution.py:28
  65.8 0.1 add_up_through.1.x
  65.9 1.6 %collective-permute-done.1.after.q_far = bf16[2048,256]{1,0:T(8,128)(2,1)S(1)} collective-permute-done((bf16[2048,256]{1,0:T(8,128)(2,1)}, bf16[2048,256]{1,0:T(8,128)(2,1)S(1)}, u32[]{:S(2)}, u32[]{:S(2)}) %collective-permute-start.1) | collective-permute-done | bytes 1048608 | tf_op jit(solution)/shard_map/ppermute | solution.py:189
  67.5 15.1 %all_to_all.21 = bf16[32,2,16,256]{3,2,1,0:T(8,128)(2,1)S(1)} all-to-all(bf16[32,2,16,256]{3,2,1,0:T(8,128)(2,1)S(1)} %hold.1), channel_id=1, replica_groups={{286,282,278,274,30,26,22,18,270,266,262,258,14,10,6,2,284,280,276,272,..., dimensions={0} | all-to-all | bytes 1048576 | tf_op jit(solution)/shard_map/all_to_all | solution.py:28
  82.6 2.6 %finish.1 = bf16[2,2048,256]{2,1,0:T(8,128)(2,1)} custom-call(s32[2]{0:T(128)S(1)} %pad_add_fusion.pos, bf16[2,16,2,16,256]{4,3,2,1,0:T(8,128)(2,1)S(1)} %bitcast.4, bf16[2,2048,256]{2,1,0:T(8,128)(2,1)S(1)} %all-to-all-done.q.q_near, bf16[2048,256]{1,0:T(8,128)(2,1)S(1)} %collective-permute-done.1.after.q_far, f32[4,8,512]{2,1,0:T(8,128)S(1)} %get-tuple-element.10.weights), custom_call_target="tpu_custom_call" | custom-call | tf_op jit(solution)/shard_map/finish/pallas_call | solution.py:220
  (3 shorter events, 0.0 us)
Async XLA Ops:
  0.0 5.4 %copy-start.2 = (f32[4,2048]{1,0:T(4,128)S(1)}, f32[4,2048]{1,0:T(4,128)}, u32[]{:S(2)}) copy-start(f32[4,2048]{1,0:T(4,128)} %c.1) | copy-start | bytes 98308
  0.0 5.4 %copy-start.3 = (f32[2048]{0:T(1024)S(1)}, f32[2048]{0:T(1024)}, u32[]{:S(2)}) copy-start(f32[2048]{0:T(1024)} %param.6) | copy-start | bytes 24580
  0.0 5.4 %copy-start.1 = (bf16[2,256,256]{2,1,0:T(8,128)(2,1)S(1)}, bf16[2,256,256]{2,1,0:T(8,128)(2,1)}, u32[]{:S(2)}) copy-start(bf16[2,256,256]{2,1,0:T(8,128)(2,1)} %t.1) | copy-start | bytes 786436
  0.0 28.9 %all-to-all-start = ((bf16[2,2048,256]{2,1,0:T(8,128)(2,1)}), bf16[2,2048,256]{2,1,0:T(8,128)(2,1)S(1)}, u32[]{:S(2)}, u32[]{:S(2)}) async-start(bf16[2,2048,256]{2,1,0:T(8,128)(2,1)} %q.1), calls=%async_computation | async-start | bytes 4194304 | tf_op jit(solution)/shard_map/all_to_all | solution.py:28
  5.4 1.6 %copy-start = (bf16[2,2048,256]{2,1,0:T(8,128)(2,1)S(1)}, bf16[2,2048,256]{2,1,0:T(8,128)(2,1)}, u32[]{:S(2)}) copy-start(bf16[2,2048,256]{2,1,0:T(8,128)(2,1)} %q.1) | copy-start | bytes 6291460
  8.9 1.0 %copy-start.4 = (bf16[2048,256]{1,0:T(8,128)(2,1)}, bf16[2048,256]{1,0:T(8,128)(2,1)S(1)}, u32[]{:S(2)}) copy-start(bf16[2048,256]{1,0:T(8,128)(2,1)S(1)} %get-tuple-element.12) | copy-start | bytes 3145732
  9.8 19.0 %collective-permute-start = (bf16[16,256]{1,0:T(8,128)(2,1)S(1)}, bf16[16,256]{1,0:T(8,128)(2,1)S(1)}, u32[]{:S(2)}, u32[]{:S(2)}) collective-permute-start(bf16[16,256]{1,0:T(8,128)(2,1)S(1)} %get-tuple-element.11), channel_id=1, source_target_pairs={{0,2},{2,0},{1,3},{3,1},{4,6},{6,4},{5,7},{7,5},{8,10},{10,8},{9,1... | collective-permute-start | bytes 24584 | tf_op jit(solution)/shard_map/ppermute | solution.py:177
  30.9 12.9 %all-to-all-start.1 = ((bf16[16,2,16,256]{3,2,1,0:T(8,128)(2,1)}), bf16[16,2,16,256]{3,2,1,0:T(8,128)(2,1)S(1)}, u32[]{:S(2)}, u32[]{:S(2)}) async-start(bf16[16,2,16,256]{3,2,1,0:T(8,128)(2,1)} %gram.1), calls=%async_computation.1 | async-start | bytes 524288 | tf_op jit(solution)/shard_map/all_to_all | solution.py:28
  38.6 28.9 %collective-permute-start.1 = (bf16[2048,256]{1,0:T(8,128)(2,1)}, bf16[2048,256]{1,0:T(8,128)(2,1)S(1)}, u32[]{:S(2)}, u32[]{:S(2)}) collective-permute-start(bf16[2048,256]{1,0:T(8,128)(2,1)} %copy-done.4), channel_id=1, source_target_pairs={{0,2},{2,0},{1,3},{3,1},{4,6},{6,4},{5,7},{7,5},{8,10},{10,8},{9,1... | collective-permute-start | bytes 3145736 | tf_op jit(solution)/shard_map/ppermute | solution.py:189
